TPU v7x, 256 devices: a whole 4x4x8 slice. The times are simulated.
256 devices in a mesh: expert: 64 (over x, z, core), dp: 4 (over y).
Axes of the slice: x: 4, y: 4, z: 8, core: 2. Of those that a mesh axis runs over, the one named last changes fastest.
Arguments:
- tokens: bfloat16 [4096, 4096], P(('expert', 'dp')), may hold values from -6 to 6
- routed_expert_index: int32 [4096, 8], P(('expert', 'dp')), may hold values from 0 to 63, all different within a row; in each aligned block of 16 rows (0 to 15, 16 to 31, ...) at most 4 rows name the same one
- routing_weight: float32 [4096, 8], P(('expert', 'dp')), may hold values from 0.05 to 0.25
- token_tenant_index: int32 [4096], P(('expert', 'dp')), may hold values from 0 to 15
- adapter_present: int32 [16, 64], replicated, may hold values 0 or 1
- gate_weight: bfloat16 [64, 4096, 1536], P('expert', None, 'dp'), may hold values from -0.09375 to 0.09375
- up_weight: bfloat16 [64, 4096, 1536], P('expert', None, 'dp'), may hold values from -0.09375 to 0.09375
- down_weight: bfloat16 [64, 1536, 4096], P('expert', 'dp'), may hold values from -0.15625 to 0.15625
- adapter_input_maps: bfloat16 [16, 64, 32, 4096], P('dp', 'expert'), may hold values from -0.09375 to 0.09375
- adapter_output_maps: bfloat16 [16, 64, 32, 1536], P('dp', 'expert'), may hold values from -1.5 to 1.5
Outputs:
- mixed_out: bfloat16 [4096, 4096], P(('expert', 'dp'))
Inputs may be any that keep to these rules, and one draw needn't show every extreme that they name: `routed_expert_index`: each row names 8 different experts. In each aligned block of 16 rows (the rows of one device) no expert is named by more than 4 rows, and in every draw some expert is named by exactly 4 rows of some block.
All inputs are finite; a program needn't handle non-finite values.
Results may differ from a plain program's by a relative error of at most 0.015.
Values may be sent and summed in bfloat16 or wider, within the bound.
No kernel may reach another device: no remote copies, remote signals or barrier semaphores. Data moves between devices by JAX's collectives and lax.ppermute only.
A program may use at most 128 MiB of HBM per device.

v0:
```python
import functools

import jax
import jax.numpy as jnp
from jax import lax
from jax.experimental import pallas as pl
from jax.experimental.pallas import tpu as pltpu
from jax.sharding import PartitionSpec as P

PIECES = 2
LANES = 128
TILE = 1024
SLOTS = 4
BF16 = jnp.bfloat16
F32 = jnp.float32


def over_dp(value, shift):
    size = lax.axis_size("dp")
    return lax.ppermute(value, "dp", [(i, (i + shift) % size) for i in range(size)])


def other_core(value):
    size = lax.axis_size("expert")
    return lax.ppermute(value, "expert", [(i, i ^ 1) for i in range(size)])


def core_major(owners):
    return [list(range(0, owners, 2)) + list(range(1, owners, 2))]


def exchange(rows, owners):
    return lax.all_to_all(
        rows,
        "expert",
        split_axis=0,
        concat_axis=0,
        axis_index_groups=core_major(owners),
        tiled=True,
    )


def accumulate_kernel(first, near, with_acts, with_low, unread, *refs):
    refs = list(refs)[unread:]
    blocks = [refs.pop(0) for _ in range(3 if near else 2)]
    if with_acts:
        gate_w, up_w = refs.pop(0), refs.pop(0)
    if with_low:
        maps = refs.pop(0)
    count = 2 * with_acts + with_low
    if first:
        notes = [refs.pop(0) for _ in range(3 if near else 1)]
        label = refs.pop()
    else:
        old, refs = refs[:count], refs[count:]
    new = refs
    h = pl.program_id(0)

    @pl.when(h == 0)
    def _():
        for i in range(count):
            new[i][...] = jnp.zeros_like(new[i]) if first else old[i][...]
        if first:
            at = (lax.broadcasted_iota(jnp.int32, (8, LANES), 1) == 0).astype(BF16)
            for b, note in enumerate(notes):
                height = note.shape[1]
                label[:, pl.ds(b * height, height)] = lax.dot_general(
                    at, note[0], (((1,), (1,)), ((), ())), preferred_element_type=F32
                )

    def add(b, rows):
        height = rows.shape[0]
        span = pl.ds(b * height, height)
        if with_acts:
            new[0][span, :] += jnp.dot(rows, gate_w[0], preferred_element_type=F32)
            new[1][span, :] += jnp.dot(rows, up_w[0], preferred_element_type=F32)
        if with_low:
            new[-1][:, span] += lax.dot_general(
                maps[...], rows, (((1,), (1,)), ((), ())), preferred_element_type=F32
            )

    if near:
        for b, block in enumerate(blocks):
            add(b, block[0])
    else:
        add(0, jnp.where(h == 0, blocks[0][0], blocks[1][0]))


def accumulate(
    piece, step, near, blocks, sums, gate_weight, up_weight, maps, with_acts, with_low, after=()
):
    height = blocks[0].shape[1]
    total = (3 if near else 1) * height
    hid = gate_weight.shape[2]
    first = piece == 0
    if near:
        block_spec = pl.BlockSpec((1, height, step), lambda h: (h, 0, 0))
    else:
        block_spec = pl.BlockSpec((1, height, step), lambda h: (0, 0, 0))
    weight_spec = pl.BlockSpec((1, step, hid), lambda h: (0, h * PIECES + piece, 0))
    map_spec = pl.BlockSpec((maps.shape[0], step), lambda h: (0, h * PIECES + piece))
    operands, specs = [*after, *blocks], [block_spec] * len(blocks)
    specs = [pl.BlockSpec(memory_space=pl.ANY)] * len(after) + specs
    shapes = []
    flops = 0
    if with_acts:
        operands += [gate_weight, up_weight]
        specs += [weight_spec] * 2
        shapes += [(total, hid)] * 2
        flops += 2 * total * 2 * step * 2 * hid
    if with_low:
        operands.append(maps)
        specs.append(map_spec)
        shapes.append((maps.shape[0], total))
        flops += 2 * total * 2 * step * maps.shape[0]
    sum_specs = [pl.BlockSpec(shape, lambda h: (0, 0)) for shape in shapes]
    aliases = {}
    if first:
        noted = blocks if near else blocks[:1]
        operands += noted
        specs += [pl.BlockSpec((1, height, LANES), lambda h: (0, 0, step // LANES))] * len(noted)
        shapes.append((8, total))
        sum_specs.append(pl.BlockSpec((8, total), lambda h: (0, 0)))
    else:
        aliases = {len(operands) + i: i for i in range(len(shapes))}
        operands += list(sums)
        specs += sum_specs
    moved = 4 * total * step + sum(2 * 4 * a * b for a, b in shapes)
    return pl.pallas_call(
        functools.partial(accumulate_kernel, first, near, with_acts, with_low, len(after)),
        grid=(2,),
        in_specs=specs,
        out_specs=tuple(sum_specs),
        out_shape=tuple(jax.ShapeDtypeStruct(shape, F32) for shape in shapes),
        input_output_aliases=aliases,
        cost_estimate=pl.CostEstimate(flops=flops, bytes_accessed=moved, transcendentals=0),
        compiler_params=pltpu.CompilerParams(vmem_limit_bytes=40 * 2**20),
    )(*operands)


def hidden_kernel(gate_ref, up_ref, low_ref, tenant_ref, gate_b_ref, up_b_ref, *outs):
    low = low_ref[...]
    half = low.shape[0] // 2
    tenants = gate_b_ref.shape[0] // half
    wide = low.shape[1]
    owner = lax.broadcasted_iota(jnp.int32, (tenants * half, wide), 0) // half
    hit = owner == tenant_ref[...]
    zero = jnp.zeros((), F32)

    def spread(part):
        tall = jnp.concatenate([part] * tenants, axis=0)
        return jnp.where(hit, tall, zero).astype(BF16)

    def product(part, maps):
        return lax.dot_general(
            spread(part), maps, (((0,), (0,)), ((), ())), preferred_element_type=F32
        )

    gate = gate_ref[...] + product(low[:half], gate_b_ref[...])
    up = up_ref[...] + product(low[half:], up_b_ref[...])
    hidden = (gate / (1.0 + jnp.exp(-gate)) * up).astype(BF16)
    height = outs[0].shape[0]
    for i, out in enumerate(outs):
        out[...] = hidden[i * height : (i + 1) * height]


def hidden_blocks(count, gate, up, low, tenants, gate_b, up_b):
    total, hid = gate.shape
    shape = jax.ShapeDtypeStruct((total // count, hid), BF16)
    return pl.pallas_call(
        hidden_kernel,
        out_shape=(shape,) * count,
        cost_estimate=pl.CostEstimate(
            flops=4 * total * hid * gate_b.shape[0], bytes_accessed=9 * total * hid, transcendentals=total * hid
        ),
        compiler_params=pltpu.CompilerParams(vmem_limit_bytes=40 * 2**20),
    )(gate, up, low, tenants, gate_b, up_b)


def product(hidden, weight):
    return jnp.dot(hidden[...], weight[0], preferred_element_type=F32)


def down_cost(blocks, height, hid, step):
    return pl.CostEstimate(
        flops=4 * blocks * height * hid * step,
        bytes_accessed=6 * blocks * height * step + 4 * hid * step,
        transcendentals=0,
    )


def weight_tile(piece, step, hid):
    tiles = step // TILE
    return pl.BlockSpec(
        (1, hid, TILE), lambda h, t: (0, 0, h * PIECES * tiles + piece * tiles + t)
    )


def rows_kernel(onehot, part, after, out):
    out[...] = jnp.dot(onehot[...], part[...], preferred_element_type=F32).astype(BF16)


def build_rows(onehot, part, after):
    count, columns = onehot.shape[0], part.shape[1]
    whole = pl.BlockSpec(memory_space=pltpu.VMEM)
    return pl.pallas_call(
        rows_kernel,
        in_specs=[whole, whole, pl.BlockSpec(memory_space=pl.ANY)],
        out_specs=whole,
        out_shape=jax.ShapeDtypeStruct((count, columns), BF16),
        cost_estimate=pl.CostEstimate(
            flops=64 * count * columns, bytes_accessed=2 * count * columns, transcendentals=0
        ),
    )(onehot, part, after)


def split_kernel(left, right, *refs):
    refs[-2][...] = left[...]
    refs[-1][...] = right[...]


def split_halves(left, right, after):
    _, height, columns = left.shape
    shape = jax.ShapeDtypeStruct((1, height, columns), left.dtype)
    block = pl.BlockSpec((1, height, columns), lambda h: (0, 0, 0))
    return pl.pallas_call(
        split_kernel,
        grid=(1,),
        in_specs=[block, pl.BlockSpec((1, height, columns), lambda h: (1, 0, 0))]
        + [pl.BlockSpec(memory_space=pl.ANY)] * len(after),
        out_specs=(block, block),
        out_shape=(shape, shape),
        cost_estimate=pl.CostEstimate(
            flops=1, bytes_accessed=8 * height * columns, transcendentals=0
        ),
    )(left, right, *after)


def relay_kernel(hidden, weight, lower, upper):
    total = product(hidden, weight).astype(BF16)

    @pl.when(pl.program_id(0) == 0)
    def _():
        lower[...] = total

    @pl.when(pl.program_id(0) == 1)
    def _():
        upper[...] = total


def relay_blocks(piece, step, hidden, down_weight):
    height, hid = hidden.shape
    last = step // TILE - 1
    shape = jax.ShapeDtypeStruct((height, step), BF16)
    return pl.pallas_call(
        relay_kernel,
        grid=(2, step // TILE),
        in_specs=[
            pl.BlockSpec((height, hid), lambda h, t: (0, 0)),
            weight_tile(piece, step, hid),
        ],
        out_specs=(
            pl.BlockSpec((height, TILE), lambda h, t: (0, jnp.where(h == 0, t, last))),
            pl.BlockSpec((height, TILE), lambda h, t: (0, jnp.where(h == 0, 0, t))),
        ),
        out_shape=(shape, shape),
        cost_estimate=down_cost(1, height, hid, step),
    )(hidden, down_weight)


def pass_kernel(up_hidden, down_hidden, weight, lower, upper, up_out, down_out):
    h = pl.program_id(0)
    zero = jnp.zeros((), F32)
    up = product(up_hidden, weight) + jnp.where(h == 0, lower[...].astype(F32), zero)
    down = product(down_hidden, weight) + jnp.where(h == 1, upper[...].astype(F32), zero)
    up_out[0] = up.astype(BF16)
    down_out[0] = down.astype(BF16)


def pass_blocks(piece, step, up_hidden, down_hidden, down_weight, lower, upper):
    height, hid = up_hidden.shape
    whole = pl.BlockSpec((height, hid), lambda h, t: (0, 0))
    part = pl.BlockSpec((height, TILE), lambda h, t: (0, t))
    out = pl.BlockSpec((1, height, TILE), lambda h, t: (h, 0, t))
    shape = jax.ShapeDtypeStruct((2, height, step), BF16)
    return pl.pallas_call(
        pass_kernel,
        grid=(2, step // TILE),
        in_specs=[whole, whole, weight_tile(piece, step, hid), part, part],
        out_specs=(out, out),
        out_shape=(shape, shape),
        cost_estimate=down_cost(2, height, hid, step),
    )(up_hidden, down_hidden, down_weight, lower, upper)


def last_kernel(hidden, weight, left, right, *refs):
    total = product(hidden, weight) + left[0].astype(F32) + right[0].astype(F32)
    refs[-1][0] = total.astype(BF16)


def last_block(piece, step, hidden, down_weight, left, right, after):
    height, hid = hidden.shape
    block = pl.BlockSpec((1, height, TILE), lambda h, t: (h, 0, t))
    return pl.pallas_call(
        last_kernel,
        grid=(2, step // TILE),
        in_specs=[
            pl.BlockSpec((height, hid), lambda h, t: (0, 0)),
            weight_tile(piece, step, hid),
            block,
            block,
        ]
        + [pl.BlockSpec(memory_space=pl.ANY)] * len(after),
        out_specs=block,
        out_shape=jax.ShapeDtypeStruct((2, height, step), BF16),
        cost_estimate=down_cost(1, height, hid, step),
    )(hidden, down_weight, left, right, *after)


def body(
    tokens,
    routed_expert_index,
    routing_weight,
    token_tenant_index,
    adapter_present,
    gate_weight,
    up_weight,
    down_weight,
    adapter_input_maps,
    adapter_output_maps,
):
    owners = lax.axis_size("expert")
    chips = owners // 2
    tok_dev, width = tokens.shape
    picks = routed_expert_index.shape[1]
    tenants_all, experts = adapter_present.shape
    own_tenants, _, rank_doubled, _ = adapter_input_maps.shape
    hid_dev = gate_weight.shape[2]
    half = width // 2
    step = half // PIECES
    lanes = 128
    owner_idx = lax.axis_index("expert")
    plane = lax.axis_index("dp")
    core = owner_idx % 2

    notes = jnp.concatenate(
        [
            routed_expert_index,
            token_tenant_index[:, None],
            jnp.zeros((tok_dev, lanes - picks - 1), jnp.int32),
        ],
        axis=1,
    ).astype(BF16)
    lower, upper = tokens[:, :half], tokens[:, half:]
    mine = jnp.where(core == 0, lower, upper)
    theirs = jnp.where(core == 0, upper, lower)
    arrived = other_core(jnp.concatenate([notes, theirs], axis=1))
    both_notes = jnp.concatenate([notes, arrived[:, :lanes]], axis=0)
    both = jnp.concatenate([mine, arrived[:, lanes:]], axis=0)
    both_ids = both_notes[:, :picks].astype(jnp.int32)
    both_tenants = both_notes[:, picks]
    other_weight = other_core(routing_weight)
    both_weight = jnp.concatenate([routing_weight, other_weight], axis=0)

    place = jnp.arange(experts, dtype=jnp.int32)
    expert_order = (place % chips) * 2 + place // chips
    named = both_ids[:, :, None] == expert_order[None, None, :]
    member = jnp.any(named, axis=1)
    row = jnp.arange(2 * tok_dev, dtype=jnp.int32)
    earlier = (row[:, None] > row[None, :]) & (row[:, None] // tok_dev == row[None, :] // tok_dev)
    before = jnp.dot(earlier.astype(BF16), member.astype(BF16), preferred_element_type=F32)
    row_core = jnp.where(row < tok_dev, core, 1 - core)
    key = jnp.where(member, before.astype(jnp.int32) + SLOTS * row_core[:, None], -1)
    slot = jnp.arange(2 * SLOTS, dtype=jnp.int32)
    filled = key.T[:, None, :] == slot[None, :, None]
    onehot = filled.reshape(experts * 2 * SLOTS, 2 * tok_dev).astype(BF16)

    height = chips * 2 * SLOTS

    def start_piece(piece, after):
        part = both[:, piece * step : (piece + 1) * step]
        if piece == 0:
            label = jnp.broadcast_to(both_tenants[:, None], (2 * tok_dev, lanes))
            part = jnp.concatenate([part, label], axis=1)
        rows = build_rows(onehot, part, after)
        got = exchange(rows.reshape(owners, 2 * SLOTS, part.shape[1]), owners)
        return got.reshape(2, height, part.shape[1])

    def spread_piece(own, after):
        from_left = over_dp(own, 1)
        from_right = over_dp(own, -1)
        lower, upper = split_halves(from_left, from_right, after)
        across = (over_dp(lower, 1), over_dp(upper, -1))
        return (own, from_left, from_right), across, (lower, upper)

    def map_part(shift):
        at = ((plane + shift) % 4) * hid_dev
        return lax.dynamic_slice_in_dim(adapter_output_maps[:, 0], at, hid_dev, axis=2)

    out_maps = jnp.concatenate(
        [
            map_part(0),
            over_dp(map_part(1), 1),
            over_dp(map_part(-1), -1),
            over_dp(map_part(2), 2),
        ],
        axis=0,
    )
    rank = rank_doubled // 2
    gate_b = out_maps[:, :rank].reshape(tenants_all * rank, hid_dev)
    up_b = out_maps[:, rank:].reshape(tenants_all * rank, hid_dev)

    maps = adapter_input_maps.reshape(own_tenants * rank_doubled, width)
    near_sums, far_sums, far = (), (), ()
    for piece in range(PIECES):
        near, far, halves = spread_piece(start_piece(piece, notes if piece == 0 else out_maps), far)
        run = functools.partial(accumulate, piece, step)
        shared = (gate_weight, up_weight, maps)
        if piece == 0:
            *near_sums, near_label = run(True, near, near_sums, *shared, True, True, after=halves)
            *far_sums, far_label = run(False, far, far_sums, *shared, True, True)
        elif piece < PIECES - 1:
            near_sums = run(True, near, near_sums, *shared, True, True, after=halves)
            far_sums = run(False, far, far_sums, *shared, True, True)
        else:
            near_sums = run(True, near, near_sums, *shared, True, True, after=halves)
            (far_low,) = run(False, far, far_sums[2:], *shared, False, True)
            far_acts = run(False, far, far_sums[:2], *shared, True, False)
    label_row = jnp.concatenate([near_label[:1], far_label[:1]], axis=1).astype(jnp.int32)
    low = jnp.concatenate([near_sums[2], far_low], axis=1)

    live = lax.dynamic_index_in_dim(adapter_present, owner_idx, axis=1, keepdims=False)
    own_live = lax.dynamic_slice_in_dim(live, plane * own_tenants, own_tenants)
    own_ids = plane * own_tenants + jnp.arange(own_tenants, dtype=jnp.int32)
    chosen = (label_row == own_ids[:, None]) & (own_live[:, None] != 0)
    low_own = jnp.sum(
        jnp.where(chosen[:, None, :], low.reshape(own_tenants, rank_doubled, 4 * height), 0.0),
        axis=0,
    ).astype(BF16)
    quarters = [low_own[:, i * height : (i + 1) * height] for i in range(4)]

    def arranged(order):
        return jnp.concatenate([quarters[i] for i in order], axis=1)

    low_rank = (
        low_own.astype(F32)
        + over_dp(arranged((2, 0, 3, 1)), 1).astype(F32)
        + over_dp(arranged((1, 3, 0, 2)), -1).astype(F32)
        + over_dp(arranged((3, 2, 1, 0)), 2).astype(F32)
    )
    away = (label_row // own_tenants - plane) % 4
    group = jnp.where(away == 0, 0, jnp.where(away == 3, 1, away + 1))
    label_rel = group * own_tenants + label_row % own_tenants
    split = 3 * height
    hidden_far = hidden_blocks(
        1, *far_acts, low_rank[:, split:], label_rel[:, split:], gate_b, up_b
    )
    hidden_near = hidden_blocks(
        3, *near_sums[:2], low_rank[:, :split], label_rel[:, :split], gate_b, up_b
    )

    scale = jnp.sum(jnp.where(named, both_weight[:, :, None], 0.0), axis=1)
    mix = jnp.where(filled, scale.T[:, None, :], 0.0).reshape(experts * 2 * SLOTS, 2 * tok_dev)
    mix_hi = lax.optimization_barrier(mix.astype(BF16))
    mix_lo = (mix - mix_hi.astype(F32)).astype(BF16)

    relays = [relay_blocks(piece, step, hidden_far[0], down_weight) for piece in range(PIECES)]
    relayed = [(over_dp(lower, 1), over_dp(upper, -1)) for lower, upper in relays]
    passed = [
        pass_blocks(piece, step, hidden_near[2], hidden_near[1], down_weight, *relayed[piece])
        for piece in range(PIECES)
    ]

    def return_piece(piece):
        up_sum, down_sum = passed[piece]
        after = relayed[piece + 1] if piece + 1 < PIECES else ()
        total = last_block(
            piece, step, hidden_near[0], down_weight, over_dp(up_sum, 1), over_dp(down_sum, -1), after
        )
        back = exchange(total.reshape(owners, 2 * SLOTS, step), owners)
        back = back.reshape(owners * 2 * SLOTS, step)
        contract = (((0,), (0,)), ((), ()))
        return (
            lax.dot_general(mix_hi, back, contract, preferred_element_type=F32)
            + lax.dot_general(mix_lo, back, contract, preferred_element_type=F32)
        ).astype(BF16)

    mixed = jnp.concatenate([return_piece(piece) for piece in range(PIECES)], axis=1)
    kept, sent = mixed[:tok_dev], mixed[tok_dev:]
    came = other_core(sent)
    return jnp.where(
        core == 0,
        jnp.concatenate([kept, came], axis=1),
        jnp.concatenate([came, kept], axis=1),
    )


def solution(mesh):
    placed = (
        P(("expert", "dp"), None),
        P(("expert", "dp"), None),
        P(("expert", "dp"), None),
        P(("expert", "dp")),
        P(),
        P("expert", None, "dp"),
        P("expert", None, "dp"),
        P("expert", "dp", None),
        P("dp", "expert", None, None),
        P("dp", "expert", None, None),
    )
    return jax.shard_map(
        body, mesh=mesh, in_specs=placed, out_specs=P(("expert", "dp"), None), check_vma=False
    )
```

profile of v0, /device:TPU:1, one launch (start us, length us, event | category | flops | bytes accessed | tf_op | source)
XLA Modules:
  0.0 314.0 jit_solution(8489696185190023311)
XLA Ops:
  2.5 3.3 %collective-permute-start = (bf16[16,2176]{1,0:T(8,128)(2,1)S(1)}, bf16[16,2176]{1,0:T(8,128)(2,1)S(1)}, u32[]{:S(2)}, u32[]{:S(2)}) collective-permute-start(bf16[16,2176]{1,0:T(8,128)(2,1)S(1)} %concatenate.65), channel_id=1, source_target_pairs={{0,4},{4,0},{8,12},{12,8},{16,20},{20,16},{24,28},{28,24},{32,36},... | collective-permute-start | bytes 208904 | tf_op jit(solution)/shard_map/ppermute | solution.py:25
  8.9 2.4 shard_map.101
  11.3 10.5 %all-to-all-start.1 = ((bf16[64,8,1152]{2,1,0:T(8,128)(2,1)}), bf16[64,8,1152]{2,1,0:T(8,128)(2,1)}, u32[]{:S(2)}, u32[]{:S(2)}) async-start(bf16[64,8,1152]{2,1,0:T(8,128)(2,1)} %bitcast.65), calls=%async_computation.1 | async-start | bytes 2359296 | tf_op jit(solution)/shard_map/all_to_all | solution.py:33
  21.9 1.4 collective-permute-start.2
  23.3 2.6 collective-permute-start.4
  25.9 1.1 collective-permute-start.3
  27.6 3.0 collective-permute-done.4
  31.5 2.3 shard_map.100
  33.8 19.9 %all-to-all-done.1 = bf16[64,8,1152]{2,1,0:T(8,128)(2,1)} async-done(((bf16[64,8,1152]{2,1,0:T(8,128)(2,1)}), bf16[64,8,1152]{2,1,0:T(8,128)(2,1)}, u32[]{:S(2)}, u32[]{:S(2)}) %all-to-all-start.1) | async-done | bytes 1179680 | tf_op jit(solution)/shard_map/all_to_all | solution.py:33
  53.7 6.4 %all-to-all-start = ((bf16[64,8,1024]{2,1,0:T(8,128)(2,1)}), bf16[64,8,1024]{2,1,0:T(8,128)(2,1)}, u32[]{:S(2)}, u32[]{:S(2)}) async-start(bf16[64,8,1024]{2,1,0:T(8,128)(2,1)} %bitcast.68), calls=%async_computation | async-start | bytes 2097152 | tf_op jit(solution)/shard_map/all_to_all | solution.py:33
  60.1 2.8 collective-permute-start.8
  62.9 26.7 %all-to-all-done = bf16[64,8,1024]{2,1,0:T(8,128)(2,1)} async-done(((bf16[64,8,1024]{2,1,0:T(8,128)(2,1)}), bf16[64,8,1024]{2,1,0:T(8,128)(2,1)}, u32[]{:S(2)}, u32[]{:S(2)}) %all-to-all-start) | async-done | bytes 1048608 | tf_op jit(solution)/shard_map/all_to_all | solution.py:33
  89.6 2.7 collective-permute-start.6
  92.3 1.5 fusion.29
  94.3 2.5 shard_map.102
  96.8 2.7 collective-permute-start.10
  100.6 1.2 copy-done.3
  103.9 6.7 %shard_map.104 = (f32[768,384]{1,0:T(8,128)S(1)}, f32[768,384]{1,0:T(8,128)S(1)}, f32[128,768]{1,0:T(8,128)S(1)}, f32[8,768]{1,0:T(8,128)S(1)}) custom-call(bf16[1,256,1152]{2,1,0:T(8,128)(2,1)S(1)} %copy-done.26, bf16[1,256,1152]{2,1,0:T(8,128)(2,1)S(1)} %copy-done.25, bf16[2,256,1152]{2,1,0:T(8,128)(2,1)} %bitcast.12.refs_2_.refs_8_, ...), custom_call_target="tpu_custom_call" | custom-call | flops 2818572288 | bytes 8699904 | tf_op jit(solution)/shard_map/pallas_call | solution.py:129
  112.4 1.2 fusion.37
  113.6 16.1 %collective-permute-done.9.refs_0_.refs_5_ = bf16[1,256,1152]{2,1,0:T(8,128)(2,1)S(1)} collective-permute-done((bf16[1,256,1152]{2,1,0:T(8,128)(2,1)}, bf16[1,256,1152]{2,1,0:T(8,128)(2,1)S(1)}, u32[]{:S(2)}, u32[]{:S(2)}) %collective-permute-start.9) | collective-permute-done | bytes 589856 | tf_op jit(solution)/shard_map/ppermute | solution.py:20
  129.7 2.0 shard_map.106
  134.6 2.3 shard_map.103
  136.8 2.7 collective-permute-start.12
  141.7 1.9 copy-done.2
  143.6 1.2 copy-done.4
  144.8 1.3 copy-done.7
  146.1 1.3 copy-done.11
  150.5 6.2 %shard_map.105 = (f32[768,384]{1,0:T(8,128)S(1)}, f32[768,384]{1,0:T(8,128)S(1)}, f32[128,768]{1,0:T(8,128)S(1)}) custom-call(bf16[1,256,1024]{2,1,0:T(8,128)(2,1)S(1)} %copy-done.28, bf16[1,256,1024]{2,1,0:T(8,128)(2,1)S(1)} %copy-done.27, bf16[2,256,1024]{2,1,0:T(8,128)(2,1)} %bitcast.10.refs_2_, ...), custom_call_target="tpu_custom_call", output_to_operand_aliasing={{0}: (8, {}), {1}: (9, {}), {2}: (10, {})} | custom-call | flops 2818572288 | bytes 8650752 | tf_op jit(solution)/shard_map/pallas_call | solution.py:129
  158.3 1.2 collective-permute-start.15
  159.5 1.5 collective-permute-start.14
  161.0 1.5 shard_map.109
  165.0 3.3 %shard_map.111 = (bf16[256,1024]{1,0:T(8,128)(2,1)}, bf16[256,1024]{1,0:T(8,128)(2,1)}) custom-call(bf16[256,384]{1,0:T(8,128)(2,1)} %copy-done.15, bf16[1,384,4096]{2,1,0:T(8,128)(2,1)} %weight.11), custom_call_target="tpu_custom_call" | custom-call | flops 402653184 | bytes 3145728 | tf_op jit(solution)/shard_map/pallas_call | solution.py:255
  169.1 1.9 collective-permute-start.17
  173.9 5.0 %collective-permute-done.16.lower = bf16[256,1024]{1,0:T(8,128)(2,1)S(1)} collective-permute-done((bf16[256,1024]{1,0:T(8,128)(2,1)}, bf16[256,1024]{1,0:T(8,128)(2,1)S(1)}, u32[]{:S(2)}, u32[]{:S(2)}) %collective-permute-start.16) | collective-permute-done | bytes 524320 | tf_op jit(solution)/shard_map/ppermute | solution.py:20
  179.7 3.8 %shard_map.112 = (bf16[2,256,1024]{2,1,0:T(8,128)(2,1)}, bf16[2,256,1024]{2,1,0:T(8,128)(2,1)}) custom-call(bf16[256,384]{1,0:T(8,128)(2,1)} %copy-done.23, bf16[256,384]{1,0:T(8,128)(2,1)} %copy-done.22, bf16[1,384,4096]{2,1,0:T(8,128)(2,1)} %weight.11, bf16[256,1024]{1,0:T(8,128)(2,1)} %copy-done.39, bf16[256,1024]{1,0:T(8,128)(2,1)} %collective-permute-done.17.upper), custom_call_target="tpu_custom_call" | custom-call | flops 805306368 | bytes 4718592 | tf_op jit(solution)/shard_map/pallas_call | solution.py:286
  183.5 2.7 collective-permute-start.19
  186.2 3.2 %shard_map.113 = (bf16[256,1024]{1,0:T(8,128)(2,1)}, bf16[256,1024]{1,0:T(8,128)(2,1)}) custom-call(bf16[256,384]{1,0:T(8,128)(2,1)} %copy-done.15, bf16[1,384,4096]{2,1,0:T(8,128)(2,1)} %weight.11), custom_call_target="tpu_custom_call" | custom-call | flops 402653184 | bytes 3145728 | tf_op jit(solution)/shard_map/pallas_call | solution.py:255
  189.4 2.7 collective-permute-start.21
  192.0 23.6 %collective-permute-done.20.refs_0_.lower = bf16[256,1024]{1,0:T(8,128)(2,1)S(1)} collective-permute-done((bf16[256,1024]{1,0:T(8,128)(2,1)}, bf16[256,1024]{1,0:T(8,128)(2,1)S(1)}, u32[]{:S(2)}, u32[]{:S(2)}) %collective-permute-start.20) | collective-permute-done | bytes 524320 | tf_op jit(solution)/shard_map/ppermute | solution.py:20
  217.4 3.4 %shard_map.114 = bf16[2,256,1024]{2,1,0:T(8,128)(2,1)} custom-call(bf16[256,384]{1,0:T(8,128)(2,1)} %copy-done.24, bf16[1,384,4096]{2,1,0:T(8,128)(2,1)} %weight.11, bf16[2,256,1024]{2,1,0:T(8,128)(2,1)} %copy-done.33, bf16[2,256,1024]{2,1,0:T(8,128)(2,1)} %copy-done.34, bf16[256,1024]{1,0:T(8,128)(2,1)} %copy-done.31, bf16[256,1024]{1,0:T(8,128)(2,1)} %copy-done.32), custom_call_target="tpu_custom_call" | custom-call | flops 402653184 | bytes 3145728 | tf_op jit(solution)/shard_map/pallas_call | solution.py:304
  220.8 13.9 %all-to-all-start.2 = ((bf16[64,8,1024]{2,1,0:T(8,128)(2,1)}), bf16[64,8,1024]{2,1,0:T(8,128)(2,1)S(1)}, u32[]{:S(2)}, u32[]{:S(2)}) async-start(bf16[64,8,1024]{2,1,0:T(8,128)(2,1)} %bitcast.66), calls=%async_computation.2 | async-start | bytes 2097152 | tf_op jit(solution)/shard_map/all_to_all | solution.py:33
  234.7 3.9 %shard_map.115 = (bf16[2,256,1024]{2,1,0:T(8,128)(2,1)}, bf16[2,256,1024]{2,1,0:T(8,128)(2,1)}) custom-call(bf16[256,384]{1,0:T(8,128)(2,1)} %copy-done.23, bf16[256,384]{1,0:T(8,128)(2,1)} %copy-done.22, bf16[1,384,4096]{2,1,0:T(8,128)(2,1)} %weight.11, bf16[256,1024]{1,0:T(8,128)(2,1)} %copy-done.31, bf16[256,1024]{1,0:T(8,128)(2,1)} %copy-done.32), custom_call_target="tpu_custom_call" | custom-call | flops 805306368 | bytes 4718592 | tf_op jit(solution)/shard_map/pallas_call | solution.py:286
  238.6 2.7 collective-permute-start.23
  241.2 23.1 %collective-permute-done.22.left = bf16[2,256,1024]{2,1,0:T(8,128)(2,1)S(1)} collective-permute-done((bf16[2,256,1024]{2,1,0:T(8,128)(2,1)}, bf16[2,256,1024]{2,1,0:T(8,128)(2,1)S(1)}, u32[]{:S(2)}, u32[]{:S(2)}) %collective-permute-start.22) | collective-permute-done | bytes 1048608 | tf_op jit(solution)/shard_map/ppermute | solution.py:20
  266.3 3.4 %shard_map.116 = bf16[2,256,1024]{2,1,0:T(8,128)(2,1)} custom-call(bf16[256,384]{1,0:T(8,128)(2,1)} %copy-done.24, bf16[1,384,4096]{2,1,0:T(8,128)(2,1)} %weight.11, bf16[2,256,1024]{2,1,0:T(8,128)(2,1)} %copy-done.35, bf16[2,256,1024]{2,1,0:T(8,128)(2,1)} %copy-done.36), custom_call_target="tpu_custom_call" | custom-call | flops 402653184 | bytes 3145728 | tf_op jit(solution)/shard_map/pallas_call | solution.py:304
  269.7 11.2 %all-to-all-start.3 = ((bf16[64,8,1024]{2,1,0:T(8,128)(2,1)}), bf16[64,8,1024]{2,1,0:T(8,128)(2,1)S(1)}, u32[]{:S(2)}, u32[]{:S(2)}) async-start(bf16[64,8,1024]{2,1,0:T(8,128)(2,1)} %bitcast.67), calls=%async_computation.3 | async-start | bytes 2097152 | tf_op jit(solution)/shard_map/all_to_all | solution.py:33
  283.5 27.0 %all-to-all-done.3 = bf16[64,8,1024]{2,1,0:T(8,128)(2,1)S(1)} async-done(((bf16[64,8,1024]{2,1,0:T(8,128)(2,1)}), bf16[64,8,1024]{2,1,0:T(8,128)(2,1)S(1)}, u32[]{:S(2)}, u32[]{:S(2)}) %all-to-all-start.3) | async-done | bytes 1048608 | tf_op jit(solution)/shard_map/all_to_all | solution.py:33
  311.3 1.1 collective-permute-start.24
  (177 shorter events, 37.7 us)
Async XLA Ops:
  2.5 4.2 %collective-permute-start = (bf16[16,2176]{1,0:T(8,128)(2,1)S(1)}, bf16[16,2176]{1,0:T(8,128)(2,1)S(1)}, u32[]{:S(2)}, u32[]{:S(2)}) collective-permute-start(bf16[16,2176]{1,0:T(8,128)(2,1)S(1)} %concatenate.65), channel_id=1, source_target_pairs={{0,4},{4,0},{8,12},{12,8},{16,20},{20,16},{24,28},{28,24},{32,36},... | collective-permute-start | bytes 208904 | tf_op jit(solution)/shard_map/ppermute | solution.py:25
  7.4 3.9 %copy-start.37 = (s32[64,32]{1,0:T(8,128)}, s32[64,32]{1,0:T(8,128)S(1)}, u32[]{:S(2)}) copy-start(s32[64,32]{1,0:T(8,128)S(1)} %copy.30) | copy-start | bytes 24580
  11.3 10.6 %copy-start.40 = (bf16[4,1,32,1536]{3,2,1,0:T(8,128)(2,1)S(1)}, bf16[4,1,32,1536]{3,2,1,0:T(8,128)(2,1)}, u32[]{:S(2)}) copy-start(bf16[4,1,32,1536]{3,2,1,0:T(8,128)(2,1)} %param.19) | copy-start | bytes 1179652
  11.3 42.4 %all-to-all-start.1 = ((bf16[64,8,1152]{2,1,0:T(8,128)(2,1)}), bf16[64,8,1152]{2,1,0:T(8,128)(2,1)}, u32[]{:S(2)}, u32[]{:S(2)}) async-start(bf16[64,8,1152]{2,1,0:T(8,128)(2,1)} %bitcast.65), calls=%async_computation.1 | async-start | bytes 2359296 | tf_op jit(solution)/shard_map/all_to_all | solution.py:33
  21.9 5.7 %collective-permute-start.2 = (bf16[4,32,384]{2,1,0:T(8,128)(2,1)S(1)}, bf16[4,32,384]{2,1,0:T(8,128)(2,1)S(1)}, u32[]{:S(2)}, u32[]{:S(2)}) collective-permute-start(bf16[4,32,384]{2,1,0:T(8,128)(2,1)S(1)} %get-tuple-element.64), channel_id=1, source_target_pairs={{0,1},{1,2},{2,3},{3,0},{4,5},{5,6},{6,7},{7,4},{8,9},{9,10},{10,1... | collective-permute-start | bytes 294920 | tf_op jit(solution)/shard_map/ppermute | solution.py:20
  23.3 7.3 %collective-permute-start.4 = (bf16[4,32,384]{2,1,0:T(8,128)(2,1)S(1)}, bf16[4,32,384]{2,1,0:T(8,128)(2,1)S(1)}, u32[]{:S(2)}, u32[]{:S(2)}) collective-permute-start(bf16[4,32,384]{2,1,0:T(8,128)(2,1)S(1)} %get-tuple-element.65), channel_id=1, source_target_pairs={{0,2},{1,3},{2,0},{3,1},{4,6},{5,7},{6,4},{7,5},{8,10},{9,11},{10,... | collective-permute-start | bytes 294920 | tf_op jit(solution)/shard_map/ppermute | solution.py:20
  25.9 4.7 %collective-permute-start.3 = (bf16[4,32,384]{2,1,0:T(8,128)(2,1)S(1)}, bf16[4,32,384]{2,1,0:T(8,128)(2,1)S(1)}, u32[]{:S(2)}, u32[]{:S(2)}) collective-permute-start(bf16[4,32,384]{2,1,0:T(8,128)(2,1)S(1)} %get-tuple-element.66), channel_id=1, source_target_pairs={{0,3},{1,0},{2,1},{3,2},{4,7},{5,4},{6,5},{7,6},{8,11},{9,8},{10,9... | collective-permute-start | bytes 294920 | tf_op jit(solution)/shard_map/ppermute | solution.py:20
  53.7 35.9 %all-to-all-start = ((bf16[64,8,1024]{2,1,0:T(8,128)(2,1)}), bf16[64,8,1024]{2,1,0:T(8,128)(2,1)}, u32[]{:S(2)}, u32[]{:S(2)}) async-start(bf16[64,8,1024]{2,1,0:T(8,128)(2,1)} %bitcast.68), calls=%async_computation | async-start | bytes 2097152 | tf_op jit(solution)/shard_map/all_to_all | solution.py:33
  60.1 34.2 %collective-permute-start.8 = (bf16[2,256,1152]{2,1,0:T(8,128)(2,1)}, bf16[2,256,1152]{2,1,0:T(8,128)(2,1)}, u32[]{:S(2)}, u32[]{:S(2)}) collective-permute-start(bf16[2,256,1152]{2,1,0:T(8,128)(2,1)} %bitcast.12.refs_2_.refs_8_), channel_id=1, source_target_pairs={{0,3},{1,0},{2,1},{3,2},{4,7},{5,4},{6,5},{7,6},{8,11},{9,8},{10,9... | collective-permute-start | bytes 3538952 | tf_op jit(solution)/shard_map/ppermute | solution.py:20
  62.9 31.4 %collective-permute-start.7 = (bf16[2,256,1152]{2,1,0:T(8,128)(2,1)}, bf16[2,256,1152]{2,1,0:T(8,128)(2,1)}, u32[]{:S(2)}, u32[]{:S(2)}) collective-permute-start(bf16[2,256,1152]{2,1,0:T(8,128)(2,1)} %bitcast.12.refs_2_.refs_8_), channel_id=1, source_target_pairs={{0,1},{1,2},{2,3},{3,0},{4,5},{5,6},{6,7},{7,4},{8,9},{9,10},{10,1... | collective-permute-start | bytes 3538952 | tf_op jit(solution)/shard_map/ppermute | solution.py:20
  89.6 45.0 %collective-permute-start.6 = (bf16[2,256,1024]{2,1,0:T(8,128)(2,1)}, bf16[2,256,1024]{2,1,0:T(8,128)(2,1)}, u32[]{:S(2)}, u32[]{:S(2)}) collective-permute-start(bf16[2,256,1024]{2,1,0:T(8,128)(2,1)} %bitcast.10.refs_2_), channel_id=1, source_target_pairs={{0,3},{1,0},{2,1},{3,2},{4,7},{5,4},{6,5},{7,6},{8,11},{9,8},{10,9... | collective-permute-start | bytes 3145736 | tf_op jit(solution)/shard_map/ppermute | solution.py:20
  92.3 42.2 %collective-permute-start.5 = (bf16[2,256,1024]{2,1,0:T(8,128)(2,1)}, bf16[2,256,1024]{2,1,0:T(8,128)(2,1)}, u32[]{:S(2)}, u32[]{:S(2)}) collective-permute-start(bf16[2,256,1024]{2,1,0:T(8,128)(2,1)} %bitcast.10.refs_2_), channel_id=1, source_target_pairs={{0,1},{1,2},{2,3},{3,0},{4,5},{5,6},{6,7},{7,4},{8,9},{9,10},{10,1... | collective-permute-start | bytes 3145736 | tf_op jit(solution)/shard_map/ppermute | solution.py:20
  94.3 6.2 %copy-start = (bf16[1,4096,384]{2,1,0:T(8,128)(2,1)S(1)}, bf16[1,4096,384]{2,1,0:T(8,128)(2,1)}, u32[]{:S(2)}) copy-start(bf16[1,4096,384]{2,1,0:T(8,128)(2,1)} %refs_2_.3) | copy-start | bytes 9437188
  96.8 32.9 %collective-permute-start.9 = (bf16[1,256,1152]{2,1,0:T(8,128)(2,1)}, bf16[1,256,1152]{2,1,0:T(8,128)(2,1)S(1)}, u32[]{:S(2)}, u32[]{:S(2)}) collective-permute-start(bf16[1,256,1152]{2,1,0:T(8,128)(2,1)} %get-tuple-element.33.refs_0_), channel_id=1, source_target_pairs={{0,1},{1,2},{2,3},{3,0},{4,5},{5,6},{6,7},{7,4},{8,9},{9,10},{10,1... | collective-permute-start | bytes 1769480 | tf_op jit(solution)/shard_map/ppermute | solution.py:20
  96.8 32.9 %collective-permute-start.10 = (bf16[1,256,1152]{2,1,0:T(8,128)(2,1)}, bf16[1,256,1152]{2,1,0:T(8,128)(2,1)S(1)}, u32[]{:S(2)}, u32[]{:S(2)}) collective-permute-start(bf16[1,256,1152]{2,1,0:T(8,128)(2,1)} %get-tuple-element.34.refs_1_), channel_id=1, source_target_pairs={{0,3},{1,0},{2,1},{3,2},{4,7},{5,4},{6,5},{7,6},{8,11},{9,8},{10,9... | collective-permute-start | bytes 1769480 | tf_op jit(solution)/shard_map/ppermute | solution.py:20
  103.9 25.8 %copy-start.1 = (bf16[1,4096,384]{2,1,0:T(8,128)(2,1)S(1)}, bf16[1,4096,384]{2,1,0:T(8,128)(2,1)}, u32[]{:S(2)}) copy-start(bf16[1,4096,384]{2,1,0:T(8,128)(2,1)} %refs_3_.3) | copy-start | bytes 9437188
  112.4 19.4 %copy-start.6 = (f32[768,384]{1,0:T(8,128)}, f32[768,384]{1,0:T(8,128)S(1)}, u32[]{:S(2)}) copy-start(f32[768,384]{1,0:T(8,128)S(1)} %get-tuple-element.37.refs_8_) | copy-start | bytes 3538948
  129.7 2.1 copy-start.5
  129.7 2.1 copy-start.14
  136.8 19.9 %collective-permute-start.11 = (bf16[1,256,1024]{2,1,0:T(8,128)(2,1)}, bf16[1,256,1024]{2,1,0:T(8,128)(2,1)S(1)}, u32[]{:S(2)}, u32[]{:S(2)}) collective-permute-start(bf16[1,256,1024]{2,1,0:T(8,128)(2,1)} %get-tuple-element.35.refs_0_), channel_id=1, source_target_pairs={{0,1},{1,2},{2,3},{3,0},{4,5},{5,6},{6,7},{7,4},{8,9},{9,10},{10,1... | collective-permute-start | bytes 1572872 | tf_op jit(solution)/shard_map/ppermute | solution.py:20
  136.8 19.9 %collective-permute-start.12 = (bf16[1,256,1024]{2,1,0:T(8,128)(2,1)}, bf16[1,256,1024]{2,1,0:T(8,128)(2,1)S(1)}, u32[]{:S(2)}, u32[]{:S(2)}) collective-permute-start(bf16[1,256,1024]{2,1,0:T(8,128)(2,1)} %get-tuple-element.36.refs_1_), channel_id=1, source_target_pairs={{0,3},{1,0},{2,1},{3,2},{4,7},{5,4},{6,5},{7,6},{8,11},{9,8},{10,9... | collective-permute-start | bytes 1572872 | tf_op jit(solution)/shard_map/ppermute | solution.py:20
  141.7 1.9 copy-start.2
  150.5 6.2 %copy-start.30 = (f32[128,256]{1,0:T(8,128)S(1)}, f32[128,256]{1,0:T(8,128)}, u32[]{:S(2)}) copy-start(f32[128,256]{1,0:T(8,128)} %copy-done.29) | copy-start | bytes 393220
  158.1 2.9 copy-start.19
  158.1 2.9 copy-start.21
  158.2 5.1 %collective-permute-start.13 = (bf16[32,1024]{1,0:T(8,128)(2,1)S(1)}, bf16[32,1024]{1,0:T(8,128)(2,1)S(1)}, u32[]{:S(2)}, u32[]{:S(2)}) collective-permute-start(bf16[32,1024]{1,0:T(8,128)(2,1)S(1)} %get-tuple-element.71), channel_id=1, source_target_pairs={{0,1},{1,2},{2,3},{3,0},{4,5},{5,6},{6,7},{7,4},{8,9},{9,10},{10,1... | collective-permute-start | bytes 196616 | tf_op jit(solution)/shard_map/ppermute | solution.py:20
  158.3 5.0 %collective-permute-start.15 = (bf16[32,1024]{1,0:T(8,128)(2,1)S(1)}, bf16[32,1024]{1,0:T(8,128)(2,1)S(1)}, u32[]{:S(2)}, u32[]{:S(2)}) collective-permute-start(bf16[32,1024]{1,0:T(8,128)(2,1)S(1)} %get-tuple-element.72), channel_id=1, source_target_pairs={{0,2},{1,3},{2,0},{3,1},{4,6},{5,7},{6,4},{7,5},{8,10},{9,11},{10,... | collective-permute-start | bytes 196616 | tf_op jit(solution)/shard_map/ppermute | solution.py:20
  159.5 4.4 %collective-permute-start.14 = (bf16[32,1024]{1,0:T(8,128)(2,1)S(1)}, bf16[32,1024]{1,0:T(8,128)(2,1)S(1)}, u32[]{:S(2)}, u32[]{:S(2)}) collective-permute-start(bf16[32,1024]{1,0:T(8,128)(2,1)S(1)} %get-tuple-element.73), channel_id=1, source_target_pairs={{0,3},{1,0},{2,1},{3,2},{4,7},{5,4},{6,5},{7,6},{8,11},{9,8},{10,9... | collective-permute-start | bytes 196616 | tf_op jit(solution)/shard_map/ppermute | solution.py:20
  165.0 6.0 %copy-start.44 = (s32[1,1024]{1,0:T(1,128)S(1)}, s32[1,1024]{1,0:T(1,128)}, u32[]{:S(2)}) copy-start(s32[1,1024]{1,0:T(1,128)} %copy-done.43) | copy-start | bytes 12292
  165.0 6.0 %copy-start.9 = (f32[768,384]{1,0:T(8,128)S(1)}, f32[768,384]{1,0:T(8,128)}, u32[]{:S(2)}) copy-start(f32[768,384]{1,0:T(8,128)} %copy-done.8) | copy-start | bytes 3538948
  165.0 6.0 %copy-start.13 = (f32[768,384]{1,0:T(8,128)S(1)}, f32[768,384]{1,0:T(8,128)}, u32[]{:S(2)}) copy-start(f32[768,384]{1,0:T(8,128)} %copy-done.12) | copy-start | bytes 3538948
  168.3 10.6 %collective-permute-start.16 = (bf16[256,1024]{1,0:T(8,128)(2,1)}, bf16[256,1024]{1,0:T(8,128)(2,1)S(1)}, u32[]{:S(2)}, u32[]{:S(2)}) collective-permute-start(bf16[256,1024]{1,0:T(8,128)(2,1)} %get-tuple-element.53), channel_id=1, source_target_pairs={{0,1},{1,2},{2,3},{3,0},{4,5},{5,6},{6,7},{7,4},{8,9},{9,10},{10,1... | collective-permute-start | bytes 1572872 | tf_op jit(solution)/shard_map/ppermute | solution.py:20
  169.1 9.8 %collective-permute-start.17 = (bf16[256,1024]{1,0:T(8,128)(2,1)}, bf16[256,1024]{1,0:T(8,128)(2,1)}, u32[]{:S(2)}, u32[]{:S(2)}) collective-permute-start(bf16[256,1024]{1,0:T(8,128)(2,1)} %get-tuple-element.54), channel_id=1, source_target_pairs={{0,3},{1,0},{2,1},{3,2},{4,7},{5,4},{6,5},{7,6},{8,11},{9,8},{10,9... | collective-permute-start | bytes 1572872 | tf_op jit(solution)/shard_map/ppermute | solution.py:20
  183.5 32.2 %collective-permute-start.18 = (bf16[2,256,1024]{2,1,0:T(8,128)(2,1)}, bf16[2,256,1024]{2,1,0:T(8,128)(2,1)S(1)}, u32[]{:S(2)}, u32[]{:S(2)}) collective-permute-start(bf16[2,256,1024]{2,1,0:T(8,128)(2,1)} %get-tuple-element.55), channel_id=1, source_target_pairs={{0,1},{1,2},{2,3},{3,0},{4,5},{5,6},{6,7},{7,4},{8,9},{9,10},{10,1... | collective-permute-start | bytes 3145736 | tf_op jit(solution)/shard_map/ppermute | solution.py:20
  183.5 32.2 %collective-permute-start.19 = (bf16[2,256,1024]{2,1,0:T(8,128)(2,1)}, bf16[2,256,1024]{2,1,0:T(8,128)(2,1)S(1)}, u32[]{:S(2)}, u32[]{:S(2)}) collective-permute-start(bf16[2,256,1024]{2,1,0:T(8,128)(2,1)} %get-tuple-element.56), channel_id=1, source_target_pairs={{0,3},{1,0},{2,1},{3,2},{4,7},{5,4},{6,5},{7,6},{8,11},{9,8},{10,9... | collective-permute-start | bytes 3145736 | tf_op jit(solution)/shard_map/ppermute | solution.py:20
  189.4 26.3 %collective-permute-start.20 = (bf16[256,1024]{1,0:T(8,128)(2,1)}, bf16[256,1024]{1,0:T(8,128)(2,1)S(1)}, u32[]{:S(2)}, u32[]{:S(2)}) collective-permute-start(bf16[256,1024]{1,0:T(8,128)(2,1)} %get-tuple-element.57), channel_id=1, source_target_pairs={{0,1},{1,2},{2,3},{3,0},{4,5},{5,6},{6,7},{7,4},{8,9},{9,10},{10,1... | collective-permute-start | bytes 1572872 | tf_op jit(solution)/shard_map/ppermute | solution.py:20
  189.4 26.3 %collective-permute-start.21 = (bf16[256,1024]{1,0:T(8,128)(2,1)}, bf16[256,1024]{1,0:T(8,128)(2,1)S(1)}, u32[]{:S(2)}, u32[]{:S(2)}) collective-permute-start(bf16[256,1024]{1,0:T(8,128)(2,1)} %get-tuple-element.58), channel_id=1, source_target_pairs={{0,3},{1,0},{2,1},{3,2},{4,7},{5,4},{6,5},{7,6},{8,11},{9,8},{10,9... | collective-permute-start | bytes 1572872 | tf_op jit(solution)/shard_map/ppermute | solution.py:20
  215.7 1.7 copy-start.34
  220.8 49.0 %all-to-all-start.2 = ((bf16[64,8,1024]{2,1,0:T(8,128)(2,1)}), bf16[64,8,1024]{2,1,0:T(8,128)(2,1)S(1)}, u32[]{:S(2)}, u32[]{:S(2)}) async-start(bf16[64,8,1024]{2,1,0:T(8,128)(2,1)} %bitcast.66), calls=%async_computation.2 | async-start | bytes 2097152 | tf_op jit(solution)/shard_map/all_to_all | solution.py:33
  238.6 25.8 %collective-permute-start.22 = (bf16[2,256,1024]{2,1,0:T(8,128)(2,1)}, bf16[2,256,1024]{2,1,0:T(8,128)(2,1)S(1)}, u32[]{:S(2)}, u32[]{:S(2)}) collective-permute-start(bf16[2,256,1024]{2,1,0:T(8,128)(2,1)} %get-tuple-element.59), channel_id=1, source_target_pairs={{0,1},{1,2},{2,3},{3,0},{4,5},{5,6},{6,7},{7,4},{8,9},{9,10},{10,1... | collective-permute-start | bytes 3145736 | tf_op jit(solution)/shard_map/ppermute | solution.py:20
  238.6 25.8 %collective-permute-start.23 = (bf16[2,256,1024]{2,1,0:T(8,128)(2,1)}, bf16[2,256,1024]{2,1,0:T(8,128)(2,1)S(1)}, u32[]{:S(2)}, u32[]{:S(2)}) collective-permute-start(bf16[2,256,1024]{2,1,0:T(8,128)(2,1)} %get-tuple-element.60), channel_id=1, source_target_pairs={{0,3},{1,0},{2,1},{3,2},{4,7},{5,4},{6,5},{7,6},{8,11},{9,8},{10,9... | collective-permute-start | bytes 3145736 | tf_op jit(solution)/shard_map/ppermute | solution.py:20
  269.7 11.2 %copy-start.45 = (f32[16,8]{0,1:T(8,128)S(1)}, f32[16,8]{0,1:T(8,128)}, u32[]{:S(2)}) copy-start(f32[16,8]{0,1:T(8,128)} %param.12) | copy-start | bytes 1540
  269.7 12.7 %copy-start.47 = (s32[64]{0:T(128)S(1)}, s32[64]{0:T(128)}, u32[]{:S(2)}) copy-start(s32[64]{0:T(128)} %copy-done.46) | copy-start | bytes 772
  269.7 12.9 %copy-start.38 = (s32[64,32]{1,0:T(8,128)S(1)}, s32[64,32]{1,0:T(8,128)}, u32[]{:S(2)}) copy-start(s32[64,32]{1,0:T(8,128)} %copy-done.37) | copy-start | bytes 24580
  269.7 12.9 %copy-start.42 = (s32[512]{0:T(512)S(1)}, s32[512]{0:T(512)}, u32[]{:S(2)}) copy-start(s32[512]{0:T(512)} %copy-done.41) | copy-start | bytes 6148
  269.7 40.8 %all-to-all-start.3 = ((bf16[64,8,1024]{2,1,0:T(8,128)(2,1)}), bf16[64,8,1024]{2,1,0:T(8,128)(2,1)S(1)}, u32[]{:S(2)}, u32[]{:S(2)}) async-start(bf16[64,8,1024]{2,1,0:T(8,128)(2,1)} %bitcast.67), calls=%async_computation.3 | async-start | bytes 2097152 | tf_op jit(solution)/shard_map/all_to_all | solution.py:33
  281.0 1.3 collective-permute-start.1
  311.3 2.0 collective-permute-start.24
  (29 other events, 27.3 us)
where the time goes:
time: 315 us; the launch traced here: 314 us
  waiting for transfers between devices  148 us (47%)
  starting transfers between devices  76.3 us (24%)
  Pallas kernels  48.7 us (15%)
  local copies, waits for them, and re-layouts  28.3 us (9%)
  other arithmetic  10.7 us (3%)
    all_to_all x4, waiting for transfers between devices, exchange(): lax.all_to_all(rows, 'expert', split_axis=0, concat_axis=0, axis_index_gr...  73.7 us
    ppermute x22, waiting for transfers between devices, over_dp(): lax.ppermute(value, 'dp', [(i, (i + shift) % size) for i in range(size)])  72.3 us
    all_to_all x4, starting transfers between devices, exchange(): lax.all_to_all(rows, 'expert', split_axis=0, concat_axis=0, axis_index_gr...  42 us
    ppermute x22, starting transfers between devices, over_dp(): lax.ppermute(value, 'dp', [(i, (i + shift) % size) for i in range(size)])  29.4 us
    unnamed x97, local copies, waits for them, and re-layouts  24.6 us
    pallas_call x5, Pallas kernels, accumulate(): pl.pallas_call(functools.partial(accumulate_kernel, first, near, with_act...  17.2 us
    pallas_call x2, Pallas kernels, pass_blocks(): pl.pallas_call(pass_kernel, grid=(2, step // TILE), in_specs=[whole, whol...  7.69 us
    pallas_call x2, Pallas kernels, last_block(): pl.pallas_call(last_kernel, grid=(2, step // TILE), in_specs=[pl.BlockSpe...  6.78 us
  transfers between devices with their start and end apart: 29, of which 13 were waited for; matrix products, arithmetic and copies ran while one was open for 3% of the time, Pallas kernels for 10%

commit v1 on v0

--- a/solution.py
+++ b/solution.py
@@ -40,8 +40,8 @@
     )
 
 
-def accumulate_kernel(first, near, with_acts, with_low, unread, *refs):
-    refs = list(refs)[unread:]
+def accumulate_kernel(first, near, with_acts, with_low, *refs):
+    refs = list(refs)
     blocks = [refs.pop(0) for _ in range(3 if near else 2)]
     if with_acts:
         gate_w, up_w = refs.pop(0), refs.pop(0)
@@ -86,9 +86,7 @@
         add(0, jnp.where(h == 0, blocks[0][0], blocks[1][0]))
 
 
-def accumulate(
-    piece, step, near, blocks, sums, gate_weight, up_weight, maps, with_acts, with_low, after=()
-):
+def accumulate(piece, step, near, blocks, sums, gate_weight, up_weight, maps, with_acts, with_low):
     height = blocks[0].shape[1]
     total = (3 if near else 1) * height
     hid = gate_weight.shape[2]
@@ -99,8 +97,7 @@
         block_spec = pl.BlockSpec((1, height, step), lambda h: (0, 0, 0))
     weight_spec = pl.BlockSpec((1, step, hid), lambda h: (0, h * PIECES + piece, 0))
     map_spec = pl.BlockSpec((maps.shape[0], step), lambda h: (0, h * PIECES + piece))
-    operands, specs = [*after, *blocks], [block_spec] * len(blocks)
-    specs = [pl.BlockSpec(memory_space=pl.ANY)] * len(after) + specs
+    operands, specs = list(blocks), [block_spec] * len(blocks)
     shapes = []
     flops = 0
     if with_acts:
@@ -127,7 +124,7 @@
         specs += sum_specs
     moved = 4 * total * step + sum(2 * 4 * a * b for a, b in shapes)
     return pl.pallas_call(
-        functools.partial(accumulate_kernel, first, near, with_acts, with_low, len(after)),
+        functools.partial(accumulate_kernel, first, near, with_acts, with_low),
         grid=(2,),
         in_specs=specs,
         out_specs=tuple(sum_specs),
@@ -391,7 +388,7 @@
         from_right = over_dp(own, -1)
         lower, upper = split_halves(from_left, from_right, after)
         across = (over_dp(lower, 1), over_dp(upper, -1))
-        return (own, from_left, from_right), across, (lower, upper)
+        return (own, from_left, from_right), across
 
     def map_part(shift):
         at = ((plane + shift) % 4) * hid_dev
@@ -413,17 +410,17 @@
     maps = adapter_input_maps.reshape(own_tenants * rank_doubled, width)
     near_sums, far_sums, far = (), (), ()
     for piece in range(PIECES):
-        near, far, halves = spread_piece(start_piece(piece, notes if piece == 0 else out_maps), far)
+        near, far = spread_piece(start_piece(piece, notes if piece == 0 else out_maps), far)
         run = functools.partial(accumulate, piece, step)
         shared = (gate_weight, up_weight, maps)
         if piece == 0:
-            *near_sums, near_label = run(True, near, near_sums, *shared, True, True, after=halves)
+            *near_sums, near_label = run(True, near, near_sums, *shared, True, True)
             *far_sums, far_label = run(False, far, far_sums, *shared, True, True)
         elif piece < PIECES - 1:
-            near_sums = run(True, near, near_sums, *shared, True, True, after=halves)
+            near_sums = run(True, near, near_sums, *shared, True, True)
             far_sums = run(False, far, far_sums, *shared, True, True)
         else:
-            near_sums = run(True, near, near_sums, *shared, True, True, after=halves)
+            near_sums = run(True, near, near_sums, *shared, True, True)
             (far_low,) = run(False, far, far_sums[2:], *shared, False, True)
             far_acts = run(False, far, far_sums[:2], *shared, True, False)
     label_row = jnp.concatenate([near_label[:1], far_label[:1]], axis=1).astype(jnp.int32)

time: 315 us -> 304 us (0.965)
  local copies, waits for them, and re-layouts: 28.3 us -> 20.3 us
  waiting for transfers between devices: 148 us -> 142 us
  starting transfers between devices: 76.3 us -> 80 us
    unnamed x97 -> x81, local copies, waits for them, and re-layouts: 24.6 us -> 17 us
    ppermute x22, waiting for transfers between devices: 72.3 us -> 67 us  [over_dp(): lax.ppermute(value, 'dp', [(i, (i + shift) % size) for i in range(size)])]
  transfers between devices with their start and end apart: 29 -> 29, of which waited for: 13 -> 16; matrix products, arithmetic and copies ran while one was open for 3% -> 3% of each run, Pallas kernels for 10% -> 11%
where the time goes in v1:
time: 304 us; the launch traced here: 303 us
  waiting for transfers between devices  142 us (47%)
  starting transfers between devices  80 us (26%)
  Pallas kernels  49.3 us (16%)
  local copies, waits for them, and re-layouts  20.3 us (7%)
  other arithmetic  8.68 us (3%)
    all_to_all x4, waiting for transfers between devices, exchange(): lax.all_to_all(rows, 'expert', split_axis=0, concat_axis=0, axis_index_gr...  73.6 us
    ppermute x22, waiting for transfers between devices, over_dp(): lax.ppermute(value, 'dp', [(i, (i + shift) % size) for i in range(size)])  67 us
    all_to_all x4, starting transfers between devices, exchange(): lax.all_to_all(rows, 'expert', split_axis=0, concat_axis=0, axis_index_gr...  44.9 us
    ppermute x22, starting transfers between devices, over_dp(): lax.ppermute(value, 'dp', [(i, (i + shift) % size) for i in range(size)])  30.3 us
    pallas_call x5, Pallas kernels, accumulate(): pl.pallas_call(functools.partial(accumulate_kernel, first, near, with_act...  18 us
    unnamed x81, local copies, waits for them, and re-layouts  17 us
    pallas_call x2, Pallas kernels, pass_blocks(): pl.pallas_call(pass_kernel, grid=(2, step // TILE), in_specs=[whole, whol...  7.67 us
    pallas_call x2, Pallas kernels, last_block(): pl.pallas_call(last_kernel, grid=(2, step // TILE), in_specs=[pl.BlockSpe...  6.77 us
  transfers between devices with their start and end apart: 29, of which 16 were waited for; matrix products, arithmetic and copies ran while one was open for 3% of the time, Pallas kernels for 11%

profile of v1, /device:TPU:1, one launch (start us, length us, event | category | flops | bytes accessed | tf_op | source)
XLA Modules:
  0.0 303.0 jit_solution(9365600461121303010)
XLA Ops:
  2.5 3.3 %collective-permute-start = (bf16[16,2176]{1,0:T(8,128)(2,1)S(1)}, bf16[16,2176]{1,0:T(8,128)(2,1)S(1)}, u32[]{:S(2)}, u32[]{:S(2)}) collective-permute-start(bf16[16,2176]{1,0:T(8,128)(2,1)S(1)} %concatenate.65), channel_id=1, source_target_pairs={{0,4},{4,0},{8,12},{12,8},{16,20},{20,16},{24,28},{28,24},{32,36},... | collective-permute-start | bytes 208904 | tf_op jit(solution)/shard_map/ppermute | solution.py:25
  8.9 2.4 shard_map.101
  11.3 10.5 %all-to-all-start.1 = ((bf16[64,8,1152]{2,1,0:T(8,128)(2,1)}), bf16[64,8,1152]{2,1,0:T(8,128)(2,1)}, u32[]{:S(2)}, u32[]{:S(2)}) async-start(bf16[64,8,1152]{2,1,0:T(8,128)(2,1)} %bitcast.65), calls=%async_computation.1 | async-start | bytes 2359296 | tf_op jit(solution)/shard_map/all_to_all | solution.py:33
  22.0 1.4 collective-permute-start.2
  23.3 2.6 collective-permute-start.4
  27.7 3.0 collective-permute-done.4
  31.5 2.4 shard_map.100
  33.8 19.9 %all-to-all-done.1 = bf16[64,8,1152]{2,1,0:T(8,128)(2,1)} async-done(((bf16[64,8,1152]{2,1,0:T(8,128)(2,1)}), bf16[64,8,1152]{2,1,0:T(8,128)(2,1)}, u32[]{:S(2)}, u32[]{:S(2)}) %all-to-all-start.1) | async-done | bytes 1179680 | tf_op jit(solution)/shard_map/all_to_all | solution.py:33
  53.7 6.4 %all-to-all-start = ((bf16[64,8,1024]{2,1,0:T(8,128)(2,1)}), bf16[64,8,1024]{2,1,0:T(8,128)(2,1)}, u32[]{:S(2)}, u32[]{:S(2)}) async-start(bf16[64,8,1024]{2,1,0:T(8,128)(2,1)} %bitcast.68), calls=%async_computation | async-start | bytes 2097152 | tf_op jit(solution)/shard_map/all_to_all | solution.py:33
  60.1 2.8 collective-permute-start.8
  63.0 26.7 %all-to-all-done = bf16[64,8,1024]{2,1,0:T(8,128)(2,1)} async-done(((bf16[64,8,1024]{2,1,0:T(8,128)(2,1)}), bf16[64,8,1024]{2,1,0:T(8,128)(2,1)}, u32[]{:S(2)}, u32[]{:S(2)}) %all-to-all-start) | async-done | bytes 1048608 | tf_op jit(solution)/shard_map/all_to_all | solution.py:33
  89.6 2.7 collective-permute-start.6
  92.4 1.4 fusion.29
  94.4 1.2 fusion.35
  95.6 2.3 shard_map.104
  98.0 2.7 collective-permute-start.10
  100.6 1.9 copy-done.1
  102.5 1.2 copy-done.5
  103.7 6.3 %shard_map.102 = (f32[768,384]{1,0:T(8,128)S(1)}, f32[768,384]{1,0:T(8,128)S(1)}, f32[128,768]{1,0:T(8,128)S(1)}, f32[8,768]{1,0:T(8,128)S(1)}) custom-call(bf16[2,256,1152]{2,1,0:T(8,128)(2,1)} %bitcast.13.refs_0_.refs_6_, bf16[2,256,1152]{2,1,0:T(8,128)(2,1)} %collective-permute-done.7.refs_1_.refs_7_.left, ...), custom_call_target="tpu_custom_call" | custom-call | flops 2818572288 | bytes 8699904 | tf_op jit(solution)/shard_map/pallas_call | solution.py:126
  110.0 1.2 fusion.37
  111.2 2.9 collective-permute-done.6.refs_2_.right
  114.1 3.1 %collective-permute-done.5.refs_1_.left = bf16[2,256,1024]{2,1,0:T(8,128)(2,1)} collective-permute-done((bf16[2,256,1024]{2,1,0:T(8,128)(2,1)}, bf16[2,256,1024]{2,1,0:T(8,128)(2,1)}, u32[]{:S(2)}, u32[]{:S(2)}) %collective-permute-start.5) | collective-permute-done | bytes 1048608 | tf_op jit(solution)/shard_map/ppermute | solution.py:20
  117.2 6.2 %shard_map.103 = (f32[768,384]{1,0:T(8,128)S(1)}, f32[768,384]{1,0:T(8,128)S(1)}, f32[128,768]{1,0:T(8,128)S(1)}) custom-call(bf16[2,256,1024]{2,1,0:T(8,128)(2,1)} %bitcast.10.refs_0_, bf16[2,256,1024]{2,1,0:T(8,128)(2,1)} %collective-permute-done.5.refs_1_.left, ...), custom_call_target="tpu_custom_call", output_to_operand_aliasing={{0}: (6, {}), {1}: (7, {}), {2}: (8, {})} | custom-call | flops 2818572288 | bytes 8650752 | tf_op jit(solution)/shard_map/pallas_call | solution.py:126
  126.2 3.6 %collective-permute-done.9.refs_0_.refs_5_ = bf16[1,256,1152]{2,1,0:T(8,128)(2,1)} collective-permute-done((bf16[1,256,1152]{2,1,0:T(8,128)(2,1)}, bf16[1,256,1152]{2,1,0:T(8,128)(2,1)}, u32[]{:S(2)}, u32[]{:S(2)}) %collective-permute-start.9) | collective-permute-done | bytes 589856 | tf_op jit(solution)/shard_map/ppermute | solution.py:20
  129.9 2.2 shard_map.106
  132.1 2.7 collective-permute-start.12
  134.7 1.9 copy-done.3
  136.6 1.2 copy-done.7
  137.9 3.2 %shard_map.105 = (f32[256,384]{1,0:T(8,128)S(1)}, f32[256,384]{1,0:T(8,128)S(1)}, f32[128,256]{1,0:T(8,128)S(1)}, f32[8,256]{1,0:T(8,128)S(1)}) custom-call(bf16[1,256,1152]{2,1,0:T(8,128)(2,1)} %collective-permute-done.9.refs_0_.refs_5_, bf16[1,256,1152]{2,1,0:T(8,128)(2,1)} %collective-permute-done.10.refs_1_, bf16[1,4096,384]{2,1,0:T(8,128)(2,1)S(1)} %copy-done, ...), custom_call_target="tpu_custom_call" | custom-call | flops 939524096 | bytes 2899968 | tf_op jit(solution)/shard_map/pallas_call | solution.py:126
  141.4 3.3 %collective-permute-done.11.refs_0_ = bf16[1,256,1024]{2,1,0:T(8,128)(2,1)S(1)} collective-permute-done((bf16[1,256,1024]{2,1,0:T(8,128)(2,1)}, bf16[1,256,1024]{2,1,0:T(8,128)(2,1)S(1)}, u32[]{:S(2)}, u32[]{:S(2)}) %collective-permute-start.11) | collective-permute-done | bytes 524320 | tf_op jit(solution)/shard_map/ppermute | solution.py:20
  145.7 3.5 %collective-permute-start.15 = (bf16[32,1024]{1,0:T(8,128)(2,1)S(1)}, bf16[32,1024]{1,0:T(8,128)(2,1)S(1)}, u32[]{:S(2)}, u32[]{:S(2)}) collective-permute-start(bf16[32,1024]{1,0:T(8,128)(2,1)S(1)} %get-tuple-element.72), channel_id=1, source_target_pairs={{0,2},{1,3},{2,0},{3,1},{4,6},{5,7},{6,4},{7,5},{8,10},{9,11},{10,... | collective-permute-start | bytes 196616 | tf_op jit(solution)/shard_map/ppermute | solution.py:20
  149.2 1.6 shard_map.109
  153.4 3.3 %shard_map.111 = (bf16[256,1024]{1,0:T(8,128)(2,1)}, bf16[256,1024]{1,0:T(8,128)(2,1)}) custom-call(bf16[256,384]{1,0:T(8,128)(2,1)} %copy-done.13, bf16[1,384,4096]{2,1,0:T(8,128)(2,1)} %weight.11), custom_call_target="tpu_custom_call" | custom-call | flops 402653184 | bytes 3145728 | tf_op jit(solution)/shard_map/pallas_call | solution.py:252
  156.7 2.7 collective-permute-start.17
  162.3 3.9 %collective-permute-done.16.lower = bf16[256,1024]{1,0:T(8,128)(2,1)S(1)} collective-permute-done((bf16[256,1024]{1,0:T(8,128)(2,1)}, bf16[256,1024]{1,0:T(8,128)(2,1)S(1)}, u32[]{:S(2)}, u32[]{:S(2)}) %collective-permute-start.16) | collective-permute-done | bytes 524320 | tf_op jit(solution)/shard_map/ppermute | solution.py:20
  167.0 3.8 %shard_map.112 = (bf16[2,256,1024]{2,1,0:T(8,128)(2,1)}, bf16[2,256,1024]{2,1,0:T(8,128)(2,1)}) custom-call(bf16[256,384]{1,0:T(8,128)(2,1)} %copy-done.17, bf16[256,384]{1,0:T(8,128)(2,1)} %copy-done.16, bf16[1,384,4096]{2,1,0:T(8,128)(2,1)} %weight.11, bf16[256,1024]{1,0:T(8,128)(2,1)} %copy-done.27, bf16[256,1024]{1,0:T(8,128)(2,1)} %collective-permute-done.17.upper), custom_call_target="tpu_custom_call" | custom-call | flops 805306368 | bytes 4718592 | tf_op jit(solution)/shard_map/pallas_call | solution.py:283
  171.4 2.1 collective-permute-start.19
  173.5 3.2 %shard_map.113 = (bf16[256,1024]{1,0:T(8,128)(2,1)}, bf16[256,1024]{1,0:T(8,128)(2,1)}) custom-call(bf16[256,384]{1,0:T(8,128)(2,1)} %copy-done.13, bf16[1,384,4096]{2,1,0:T(8,128)(2,1)} %weight.11), custom_call_target="tpu_custom_call" | custom-call | flops 402653184 | bytes 3145728 | tf_op jit(solution)/shard_map/pallas_call | solution.py:252
  176.6 2.7 collective-permute-start.21
  179.3 22.5 %collective-permute-done.20.refs_0_.lower = bf16[256,1024]{1,0:T(8,128)(2,1)S(1)} collective-permute-done((bf16[256,1024]{1,0:T(8,128)(2,1)}, bf16[256,1024]{1,0:T(8,128)(2,1)S(1)}, u32[]{:S(2)}, u32[]{:S(2)}) %collective-permute-start.20) | collective-permute-done | bytes 524320 | tf_op jit(solution)/shard_map/ppermute | solution.py:20
  203.4 3.4 %shard_map.114 = bf16[2,256,1024]{2,1,0:T(8,128)(2,1)} custom-call(bf16[256,384]{1,0:T(8,128)(2,1)} %copy-done.18, bf16[1,384,4096]{2,1,0:T(8,128)(2,1)} %weight.11, bf16[2,256,1024]{2,1,0:T(8,128)(2,1)} %copy-done.21, bf16[2,256,1024]{2,1,0:T(8,128)(2,1)} %copy-done.22, bf16[256,1024]{1,0:T(8,128)(2,1)} %copy-done.19, bf16[256,1024]{1,0:T(8,128)(2,1)} %copy-done.20), custom_call_target="tpu_custom_call" | custom-call | flops 402653184 | bytes 3145728 | tf_op jit(solution)/shard_map/pallas_call | solution.py:301
  206.8 16.8 %all-to-all-start.2 = ((bf16[64,8,1024]{2,1,0:T(8,128)(2,1)}), bf16[64,8,1024]{2,1,0:T(8,128)(2,1)S(1)}, u32[]{:S(2)}, u32[]{:S(2)}) async-start(bf16[64,8,1024]{2,1,0:T(8,128)(2,1)} %bitcast.66), calls=%async_computation.2 | async-start | bytes 2097152 | tf_op jit(solution)/shard_map/all_to_all | solution.py:33
  223.6 3.9 %shard_map.115 = (bf16[2,256,1024]{2,1,0:T(8,128)(2,1)}, bf16[2,256,1024]{2,1,0:T(8,128)(2,1)}) custom-call(bf16[256,384]{1,0:T(8,128)(2,1)} %copy-done.17, bf16[256,384]{1,0:T(8,128)(2,1)} %copy-done.16, bf16[1,384,4096]{2,1,0:T(8,128)(2,1)} %weight.11, bf16[256,1024]{1,0:T(8,128)(2,1)} %copy-done.19, bf16[256,1024]{1,0:T(8,128)(2,1)} %copy-done.20), custom_call_target="tpu_custom_call" | custom-call | flops 805306368 | bytes 4718592 | tf_op jit(solution)/shard_map/pallas_call | solution.py:283
  227.5 2.7 collective-permute-start.23
  230.2 23.1 %collective-permute-done.22.left = bf16[2,256,1024]{2,1,0:T(8,128)(2,1)S(1)} collective-permute-done((bf16[2,256,1024]{2,1,0:T(8,128)(2,1)}, bf16[2,256,1024]{2,1,0:T(8,128)(2,1)S(1)}, u32[]{:S(2)}, u32[]{:S(2)}) %collective-permute-start.22) | collective-permute-done | bytes 1048608 | tf_op jit(solution)/shard_map/ppermute | solution.py:20
  255.3 3.4 %shard_map.116 = bf16[2,256,1024]{2,1,0:T(8,128)(2,1)} custom-call(bf16[256,384]{1,0:T(8,128)(2,1)} %copy-done.18, bf16[1,384,4096]{2,1,0:T(8,128)(2,1)} %weight.11, bf16[2,256,1024]{2,1,0:T(8,128)(2,1)} %copy-done.23, bf16[2,256,1024]{2,1,0:T(8,128)(2,1)} %copy-done.24), custom_call_target="tpu_custom_call" | custom-call | flops 402653184 | bytes 3145728 | tf_op jit(solution)/shard_map/pallas_call | solution.py:301
  258.7 11.2 %all-to-all-start.3 = ((bf16[64,8,1024]{2,1,0:T(8,128)(2,1)}), bf16[64,8,1024]{2,1,0:T(8,128)(2,1)S(1)}, u32[]{:S(2)}, u32[]{:S(2)}) async-start(bf16[64,8,1024]{2,1,0:T(8,128)(2,1)} %bitcast.67), calls=%async_computation.3 | async-start | bytes 2097152 | tf_op jit(solution)/shard_map/all_to_all | solution.py:33
  272.4 27.0 %all-to-all-done.3 = bf16[64,8,1024]{2,1,0:T(8,128)(2,1)S(1)} async-done(((bf16[64,8,1024]{2,1,0:T(8,128)(2,1)}), bf16[64,8,1024]{2,1,0:T(8,128)(2,1)S(1)}, u32[]{:S(2)}, u32[]{:S(2)}) %all-to-all-start.3) | async-done | bytes 1048608 | tf_op jit(solution)/shard_map/all_to_all | solution.py:33
  (161 shorter events, 29.2 us)
Async XLA Ops:
  2.5 4.2 %collective-permute-start = (bf16[16,2176]{1,0:T(8,128)(2,1)S(1)}, bf16[16,2176]{1,0:T(8,128)(2,1)S(1)}, u32[]{:S(2)}, u32[]{:S(2)}) collective-permute-start(bf16[16,2176]{1,0:T(8,128)(2,1)S(1)} %concatenate.65), channel_id=1, source_target_pairs={{0,4},{4,0},{8,12},{12,8},{16,20},{20,16},{24,28},{28,24},{32,36},... | collective-permute-start | bytes 208904 | tf_op jit(solution)/shard_map/ppermute | solution.py:25
  7.4 3.9 %copy-start.25 = (s32[64,32]{1,0:T(8,128)}, s32[64,32]{1,0:T(8,128)S(1)}, u32[]{:S(2)}) copy-start(s32[64,32]{1,0:T(8,128)S(1)} %copy.30) | copy-start | bytes 24580
  11.3 10.6 %copy-start.28 = (bf16[4,1,32,1536]{3,2,1,0:T(8,128)(2,1)S(1)}, bf16[4,1,32,1536]{3,2,1,0:T(8,128)(2,1)}, u32[]{:S(2)}) copy-start(bf16[4,1,32,1536]{3,2,1,0:T(8,128)(2,1)} %param.19) | copy-start | bytes 1179652
  11.3 42.4 %all-to-all-start.1 = ((bf16[64,8,1152]{2,1,0:T(8,128)(2,1)}), bf16[64,8,1152]{2,1,0:T(8,128)(2,1)}, u32[]{:S(2)}, u32[]{:S(2)}) async-start(bf16[64,8,1152]{2,1,0:T(8,128)(2,1)} %bitcast.65), calls=%async_computation.1 | async-start | bytes 2359296 | tf_op jit(solution)/shard_map/all_to_all | solution.py:33
  22.0 5.7 %collective-permute-start.2 = (bf16[4,32,384]{2,1,0:T(8,128)(2,1)S(1)}, bf16[4,32,384]{2,1,0:T(8,128)(2,1)S(1)}, u32[]{:S(2)}, u32[]{:S(2)}) collective-permute-start(bf16[4,32,384]{2,1,0:T(8,128)(2,1)S(1)} %get-tuple-element.64), channel_id=1, source_target_pairs={{0,1},{1,2},{2,3},{3,0},{4,5},{5,6},{6,7},{7,4},{8,9},{9,10},{10,1... | collective-permute-start | bytes 294920 | tf_op jit(solution)/shard_map/ppermute | solution.py:20
  23.3 7.3 %collective-permute-start.4 = (bf16[4,32,384]{2,1,0:T(8,128)(2,1)S(1)}, bf16[4,32,384]{2,1,0:T(8,128)(2,1)S(1)}, u32[]{:S(2)}, u32[]{:S(2)}) collective-permute-start(bf16[4,32,384]{2,1,0:T(8,128)(2,1)S(1)} %get-tuple-element.65), channel_id=1, source_target_pairs={{0,2},{1,3},{2,0},{3,1},{4,6},{5,7},{6,4},{7,5},{8,10},{9,11},{10,... | collective-permute-start | bytes 294920 | tf_op jit(solution)/shard_map/ppermute | solution.py:20
  26.0 4.7 %collective-permute-start.3 = (bf16[4,32,384]{2,1,0:T(8,128)(2,1)S(1)}, bf16[4,32,384]{2,1,0:T(8,128)(2,1)S(1)}, u32[]{:S(2)}, u32[]{:S(2)}) collective-permute-start(bf16[4,32,384]{2,1,0:T(8,128)(2,1)S(1)} %get-tuple-element.66), channel_id=1, source_target_pairs={{0,3},{1,0},{2,1},{3,2},{4,7},{5,4},{6,5},{7,6},{8,11},{9,8},{10,9... | collective-permute-start | bytes 294920 | tf_op jit(solution)/shard_map/ppermute | solution.py:20
  53.7 35.9 %all-to-all-start = ((bf16[64,8,1024]{2,1,0:T(8,128)(2,1)}), bf16[64,8,1024]{2,1,0:T(8,128)(2,1)}, u32[]{:S(2)}, u32[]{:S(2)}) async-start(bf16[64,8,1024]{2,1,0:T(8,128)(2,1)} %bitcast.68), calls=%async_computation | async-start | bytes 2097152 | tf_op jit(solution)/shard_map/all_to_all | solution.py:33
  60.1 35.5 %collective-permute-start.8 = (bf16[2,256,1152]{2,1,0:T(8,128)(2,1)}, bf16[2,256,1152]{2,1,0:T(8,128)(2,1)}, u32[]{:S(2)}, u32[]{:S(2)}) collective-permute-start(bf16[2,256,1152]{2,1,0:T(8,128)(2,1)} %bitcast.13.refs_0_.refs_6_), channel_id=1, source_target_pairs={{0,3},{1,0},{2,1},{3,2},{4,7},{5,4},{6,5},{7,6},{8,11},{9,8},{10,9... | collective-permute-start | bytes 3538952 | tf_op jit(solution)/shard_map/ppermute | solution.py:20
  62.9 32.7 %collective-permute-start.7 = (bf16[2,256,1152]{2,1,0:T(8,128)(2,1)}, bf16[2,256,1152]{2,1,0:T(8,128)(2,1)}, u32[]{:S(2)}, u32[]{:S(2)}) collective-permute-start(bf16[2,256,1152]{2,1,0:T(8,128)(2,1)} %bitcast.13.refs_0_.refs_6_), channel_id=1, source_target_pairs={{0,1},{1,2},{2,3},{3,0},{4,5},{5,6},{6,7},{7,4},{8,9},{9,10},{10,1... | collective-permute-start | bytes 3538952 | tf_op jit(solution)/shard_map/ppermute | solution.py:20
  89.6 24.5 %collective-permute-start.6 = (bf16[2,256,1024]{2,1,0:T(8,128)(2,1)}, bf16[2,256,1024]{2,1,0:T(8,128)(2,1)}, u32[]{:S(2)}, u32[]{:S(2)}) collective-permute-start(bf16[2,256,1024]{2,1,0:T(8,128)(2,1)} %bitcast.10.refs_0_), channel_id=1, source_target_pairs={{0,3},{1,0},{2,1},{3,2},{4,7},{5,4},{6,5},{7,6},{8,11},{9,8},{10,9... | collective-permute-start | bytes 3145736 | tf_op jit(solution)/shard_map/ppermute | solution.py:20
  92.4 24.9 %collective-permute-start.5 = (bf16[2,256,1024]{2,1,0:T(8,128)(2,1)}, bf16[2,256,1024]{2,1,0:T(8,128)(2,1)}, u32[]{:S(2)}, u32[]{:S(2)}) collective-permute-start(bf16[2,256,1024]{2,1,0:T(8,128)(2,1)} %bitcast.10.refs_0_), channel_id=1, source_target_pairs={{0,1},{1,2},{2,3},{3,0},{4,5},{5,6},{6,7},{7,4},{8,9},{9,10},{10,1... | collective-permute-start | bytes 3145736 | tf_op jit(solution)/shard_map/ppermute | solution.py:20
  94.4 6.2 %copy-start = (bf16[1,4096,384]{2,1,0:T(8,128)(2,1)S(1)}, bf16[1,4096,384]{2,1,0:T(8,128)(2,1)}, u32[]{:S(2)}) copy-start(bf16[1,4096,384]{2,1,0:T(8,128)(2,1)} %refs_2_.3) | copy-start | bytes 9437188
  97.9 31.9 %collective-permute-start.9 = (bf16[1,256,1152]{2,1,0:T(8,128)(2,1)}, bf16[1,256,1152]{2,1,0:T(8,128)(2,1)}, u32[]{:S(2)}, u32[]{:S(2)}) collective-permute-start(bf16[1,256,1152]{2,1,0:T(8,128)(2,1)} %get-tuple-element.39), channel_id=1, source_target_pairs={{0,1},{1,2},{2,3},{3,0},{4,5},{5,6},{6,7},{7,4},{8,9},{9,10},{10,1... | collective-permute-start | bytes 1769480 | tf_op jit(solution)/shard_map/ppermute | solution.py:20
  98.0 31.9 %collective-permute-start.10 = (bf16[1,256,1152]{2,1,0:T(8,128)(2,1)}, bf16[1,256,1152]{2,1,0:T(8,128)(2,1)}, u32[]{:S(2)}, u32[]{:S(2)}) collective-permute-start(bf16[1,256,1152]{2,1,0:T(8,128)(2,1)} %get-tuple-element.40), channel_id=1, source_target_pairs={{0,3},{1,0},{2,1},{3,2},{4,7},{5,4},{6,5},{7,6},{8,11},{9,8},{10,9... | collective-permute-start | bytes 1769480 | tf_op jit(solution)/shard_map/ppermute | solution.py:20
  103.7 13.5 %copy-start.2 = (bf16[1,4096,384]{2,1,0:T(8,128)(2,1)S(1)}, bf16[1,4096,384]{2,1,0:T(8,128)(2,1)}, u32[]{:S(2)}) copy-start(bf16[1,4096,384]{2,1,0:T(8,128)(2,1)} %refs_3_.7) | copy-start | bytes 9437188
  103.7 13.5 %copy-start.6 = (bf16[4,1,32,4096]{3,2,1,0:T(8,128)(2,1)S(1)}, bf16[4,1,32,4096]{3,2,1,0:T(8,128)(2,1)}, u32[]{:S(2)}) copy-start(bf16[4,1,32,4096]{3,2,1,0:T(8,128)(2,1)} %param.18) | copy-start | bytes 3145732
  132.0 12.6 %collective-permute-start.11 = (bf16[1,256,1024]{2,1,0:T(8,128)(2,1)}, bf16[1,256,1024]{2,1,0:T(8,128)(2,1)S(1)}, u32[]{:S(2)}, u32[]{:S(2)}) collective-permute-start(bf16[1,256,1024]{2,1,0:T(8,128)(2,1)} %get-tuple-element.43), channel_id=1, source_target_pairs={{0,1},{1,2},{2,3},{3,0},{4,5},{5,6},{6,7},{7,4},{8,9},{9,10},{10,1... | collective-permute-start | bytes 1572872 | tf_op jit(solution)/shard_map/ppermute | solution.py:20
  132.1 12.6 %collective-permute-start.12 = (bf16[1,256,1024]{2,1,0:T(8,128)(2,1)}, bf16[1,256,1024]{2,1,0:T(8,128)(2,1)S(1)}, u32[]{:S(2)}, u32[]{:S(2)}) collective-permute-start(bf16[1,256,1024]{2,1,0:T(8,128)(2,1)} %get-tuple-element.44), channel_id=1, source_target_pairs={{0,3},{1,0},{2,1},{3,2},{4,7},{5,4},{6,5},{7,6},{8,11},{9,8},{10,9... | collective-permute-start | bytes 1572872 | tf_op jit(solution)/shard_map/ppermute | solution.py:20
  137.8 3.4 %copy-start.33 = (f32[768]{0:T(1024)S(1)}, f32[768]{0:T(1024)}, u32[]{:S(2)}) copy-start(f32[768]{0:T(1024)} %get-tuple-element.79) | copy-start | bytes 9220
  137.8 3.4 %copy-start.38 = (pred[4]{0:T(512)(128)(4,1)S(1)}, pred[4]{0:T(512)(128)(4,1)}, u32[]{:S(2)}) copy-start(pred[4]{0:T(512)(128)(4,1)} %fusion.29) | copy-start | bytes 16
  137.8 3.4 %copy-start.39 = (s32[4]{0:T(128)S(1)}, s32[4]{0:T(128)}, u32[]{:S(2)}) copy-start(s32[4]{0:T(128)} %iota_add_fusion) | copy-start | bytes 52
  137.9 6.8 %copy-start.8 = (bf16[4,1,32,4096]{3,2,1,0:T(8,128)(2,1)S(1)}, bf16[4,1,32,4096]{3,2,1,0:T(8,128)(2,1)}, u32[]{:S(2)}) copy-start(bf16[4,1,32,4096]{3,2,1,0:T(8,128)(2,1)} %param.18) | copy-start | bytes 3145732
  137.9 7.6 %copy-start.15 = (f32[128,768]{1,0:T(8,128)S(1)}, f32[128,768]{1,0:T(8,128)}, u32[]{:S(2)}) copy-start(f32[128,768]{1,0:T(8,128)} %copy-done.14) | copy-start | bytes 1179652
  141.2 3.4 %copy-start.31 = (s32[1,1024]{1,0:T(1,128)}, s32[1,1024]{1,0:T(1,128)S(1)}, u32[]{:S(2)}) copy-start(s32[1,1024]{1,0:T(1,128)S(1)} %fusion.26) | copy-start | bytes 12292
  144.6 4.6 %copy-start.4 = (bf16[1,4096,384]{2,1,0:T(8,128)(2,1)S(1)}, bf16[1,4096,384]{2,1,0:T(8,128)(2,1)}, u32[]{:S(2)}) copy-start(bf16[1,4096,384]{2,1,0:T(8,128)(2,1)} %refs_3_.7) | copy-start | bytes 9437188
  145.6 5.2 %collective-permute-start.13 = (bf16[32,1024]{1,0:T(8,128)(2,1)S(1)}, bf16[32,1024]{1,0:T(8,128)(2,1)S(1)}, u32[]{:S(2)}, u32[]{:S(2)}) collective-permute-start(bf16[32,1024]{1,0:T(8,128)(2,1)S(1)} %get-tuple-element.71), channel_id=1, source_target_pairs={{0,1},{1,2},{2,3},{3,0},{4,5},{5,6},{6,7},{7,4},{8,9},{9,10},{10,1... | collective-permute-start | bytes 196616 | tf_op jit(solution)/shard_map/ppermute | solution.py:20
  145.7 5.9 %collective-permute-start.15 = (bf16[32,1024]{1,0:T(8,128)(2,1)S(1)}, bf16[32,1024]{1,0:T(8,128)(2,1)S(1)}, u32[]{:S(2)}, u32[]{:S(2)}) collective-permute-start(bf16[32,1024]{1,0:T(8,128)(2,1)S(1)} %get-tuple-element.72), channel_id=1, source_target_pairs={{0,2},{1,3},{2,0},{3,1},{4,6},{5,7},{6,4},{7,5},{8,10},{9,11},{10,... | collective-permute-start | bytes 196616 | tf_op jit(solution)/shard_map/ppermute | solution.py:20
  149.2 3.1 %collective-permute-start.14 = (bf16[32,1024]{1,0:T(8,128)(2,1)S(1)}, bf16[32,1024]{1,0:T(8,128)(2,1)S(1)}, u32[]{:S(2)}, u32[]{:S(2)}) collective-permute-start(bf16[32,1024]{1,0:T(8,128)(2,1)S(1)} %get-tuple-element.73), channel_id=1, source_target_pairs={{0,3},{1,0},{2,1},{3,2},{4,7},{5,4},{6,5},{7,6},{8,11},{9,8},{10,9... | collective-permute-start | bytes 196616 | tf_op jit(solution)/shard_map/ppermute | solution.py:20
  153.4 6.0 %copy-start.32 = (s32[1,1024]{1,0:T(1,128)S(1)}, s32[1,1024]{1,0:T(1,128)}, u32[]{:S(2)}) copy-start(s32[1,1024]{1,0:T(1,128)} %copy-done.31) | copy-start | bytes 12292
  153.4 6.0 %copy-start.10 = (f32[768,384]{1,0:T(8,128)S(1)}, f32[768,384]{1,0:T(8,128)}, u32[]{:S(2)}) copy-start(f32[768,384]{1,0:T(8,128)} %copy-done.9) | copy-start | bytes 3538948
  153.4 6.0 %copy-start.12 = (f32[768,384]{1,0:T(8,128)S(1)}, f32[768,384]{1,0:T(8,128)}, u32[]{:S(2)}) copy-start(f32[768,384]{1,0:T(8,128)} %copy-done.11) | copy-start | bytes 3538948
  156.7 9.5 %collective-permute-start.16 = (bf16[256,1024]{1,0:T(8,128)(2,1)}, bf16[256,1024]{1,0:T(8,128)(2,1)S(1)}, u32[]{:S(2)}, u32[]{:S(2)}) collective-permute-start(bf16[256,1024]{1,0:T(8,128)(2,1)} %get-tuple-element.53), channel_id=1, source_target_pairs={{0,1},{1,2},{2,3},{3,0},{4,5},{5,6},{6,7},{7,4},{8,9},{9,10},{10,1... | collective-permute-start | bytes 1572872 | tf_op jit(solution)/shard_map/ppermute | solution.py:20
  156.7 9.5 %collective-permute-start.17 = (bf16[256,1024]{1,0:T(8,128)(2,1)}, bf16[256,1024]{1,0:T(8,128)(2,1)}, u32[]{:S(2)}, u32[]{:S(2)}) collective-permute-start(bf16[256,1024]{1,0:T(8,128)(2,1)} %get-tuple-element.54), channel_id=1, source_target_pairs={{0,3},{1,0},{2,1},{3,2},{4,7},{5,4},{6,5},{7,6},{8,11},{9,8},{10,9... | collective-permute-start | bytes 1572872 | tf_op jit(solution)/shard_map/ppermute | solution.py:20
  170.8 31.0 %collective-permute-start.18 = (bf16[2,256,1024]{2,1,0:T(8,128)(2,1)}, bf16[2,256,1024]{2,1,0:T(8,128)(2,1)S(1)}, u32[]{:S(2)}, u32[]{:S(2)}) collective-permute-start(bf16[2,256,1024]{2,1,0:T(8,128)(2,1)} %get-tuple-element.55), channel_id=1, source_target_pairs={{0,1},{1,2},{2,3},{3,0},{4,5},{5,6},{6,7},{7,4},{8,9},{9,10},{10,1... | collective-permute-start | bytes 3145736 | tf_op jit(solution)/shard_map/ppermute | solution.py:20
  171.4 30.4 %collective-permute-start.19 = (bf16[2,256,1024]{2,1,0:T(8,128)(2,1)}, bf16[2,256,1024]{2,1,0:T(8,128)(2,1)S(1)}, u32[]{:S(2)}, u32[]{:S(2)}) collective-permute-start(bf16[2,256,1024]{2,1,0:T(8,128)(2,1)} %get-tuple-element.56), channel_id=1, source_target_pairs={{0,3},{1,0},{2,1},{3,2},{4,7},{5,4},{6,5},{7,6},{8,11},{9,8},{10,9... | collective-permute-start | bytes 3145736 | tf_op jit(solution)/shard_map/ppermute | solution.py:20
  176.6 25.1 %collective-permute-start.20 = (bf16[256,1024]{1,0:T(8,128)(2,1)}, bf16[256,1024]{1,0:T(8,128)(2,1)S(1)}, u32[]{:S(2)}, u32[]{:S(2)}) collective-permute-start(bf16[256,1024]{1,0:T(8,128)(2,1)} %get-tuple-element.57), channel_id=1, source_target_pairs={{0,1},{1,2},{2,3},{3,0},{4,5},{5,6},{6,7},{7,4},{8,9},{9,10},{10,1... | collective-permute-start | bytes 1572872 | tf_op jit(solution)/shard_map/ppermute | solution.py:20
  176.6 25.2 %collective-permute-start.21 = (bf16[256,1024]{1,0:T(8,128)(2,1)}, bf16[256,1024]{1,0:T(8,128)(2,1)S(1)}, u32[]{:S(2)}, u32[]{:S(2)}) collective-permute-start(bf16[256,1024]{1,0:T(8,128)(2,1)} %get-tuple-element.58), channel_id=1, source_target_pairs={{0,3},{1,0},{2,1},{3,2},{4,7},{5,4},{6,5},{7,6},{8,11},{9,8},{10,9... | collective-permute-start | bytes 1572872 | tf_op jit(solution)/shard_map/ppermute | solution.py:20
  206.8 51.8 %all-to-all-start.2 = ((bf16[64,8,1024]{2,1,0:T(8,128)(2,1)}), bf16[64,8,1024]{2,1,0:T(8,128)(2,1)S(1)}, u32[]{:S(2)}, u32[]{:S(2)}) async-start(bf16[64,8,1024]{2,1,0:T(8,128)(2,1)} %bitcast.66), calls=%async_computation.2 | async-start | bytes 2097152 | tf_op jit(solution)/shard_map/all_to_all | solution.py:33
  227.5 25.8 %collective-permute-start.22 = (bf16[2,256,1024]{2,1,0:T(8,128)(2,1)}, bf16[2,256,1024]{2,1,0:T(8,128)(2,1)S(1)}, u32[]{:S(2)}, u32[]{:S(2)}) collective-permute-start(bf16[2,256,1024]{2,1,0:T(8,128)(2,1)} %get-tuple-element.59), channel_id=1, source_target_pairs={{0,1},{1,2},{2,3},{3,0},{4,5},{5,6},{6,7},{7,4},{8,9},{9,10},{10,1... | collective-permute-start | bytes 3145736 | tf_op jit(solution)/shard_map/ppermute | solution.py:20
  227.5 25.8 %collective-permute-start.23 = (bf16[2,256,1024]{2,1,0:T(8,128)(2,1)}, bf16[2,256,1024]{2,1,0:T(8,128)(2,1)S(1)}, u32[]{:S(2)}, u32[]{:S(2)}) collective-permute-start(bf16[2,256,1024]{2,1,0:T(8,128)(2,1)} %get-tuple-element.60), channel_id=1, source_target_pairs={{0,3},{1,0},{2,1},{3,2},{4,7},{5,4},{6,5},{7,6},{8,11},{9,8},{10,9... | collective-permute-start | bytes 3145736 | tf_op jit(solution)/shard_map/ppermute | solution.py:20
  258.6 11.2 %copy-start.35 = (f32[16,8]{0,1:T(8,128)S(1)}, f32[16,8]{0,1:T(8,128)}, u32[]{:S(2)}) copy-start(f32[16,8]{0,1:T(8,128)} %param.12) | copy-start | bytes 1540
  258.6 12.7 %copy-start.37 = (s32[64]{0:T(128)S(1)}, s32[64]{0:T(128)}, u32[]{:S(2)}) copy-start(s32[64]{0:T(128)} %copy-done.36) | copy-start | bytes 772
  258.6 12.9 %copy-start.26 = (s32[64,32]{1,0:T(8,128)S(1)}, s32[64,32]{1,0:T(8,128)}, u32[]{:S(2)}) copy-start(s32[64,32]{1,0:T(8,128)} %copy-done.25) | copy-start | bytes 24580
  258.6 12.9 %copy-start.30 = (s32[512]{0:T(512)S(1)}, s32[512]{0:T(512)}, u32[]{:S(2)}) copy-start(s32[512]{0:T(512)} %copy-done.29) | copy-start | bytes 6148
  258.7 40.8 %all-to-all-start.3 = ((bf16[64,8,1024]{2,1,0:T(8,128)(2,1)}), bf16[64,8,1024]{2,1,0:T(8,128)(2,1)S(1)}, u32[]{:S(2)}, u32[]{:S(2)}) async-start(bf16[64,8,1024]{2,1,0:T(8,128)(2,1)} %bitcast.67), calls=%async_computation.3 | async-start | bytes 2097152 | tf_op jit(solution)/shard_map/all_to_all | solution.py:33
  269.9 1.3 collective-permute-start.1
  300.2 2.0 collective-permute-start.24
  (21 other events, 23.9 us)

commit v2 on v0

--- a/solution.py
+++ b/solution.py
@@ -389,9 +389,9 @@
     def spread_piece(own, after):
         from_left = over_dp(own, 1)
         from_right = over_dp(own, -1)
-        lower, upper = split_halves(from_left, from_right, after)
+        lower, upper = split_halves(from_left, from_right, ())
         across = (over_dp(lower, 1), over_dp(upper, -1))
-        return (own, from_left, from_right), across, (lower, upper)
+        return (own, from_left, from_right), across
 
     def map_part(shift):
         at = ((plane + shift) % 4) * hid_dev
@@ -411,19 +411,20 @@
     up_b = out_maps[:, rank:].reshape(tenants_all * rank, hid_dev)
 
     maps = adapter_input_maps.reshape(own_tenants * rank_doubled, width)
-    near_sums, far_sums, far = (), (), ()
+    near_sums, far_sums, far, waited = (), (), (), ()
     for piece in range(PIECES):
-        near, far, halves = spread_piece(start_piece(piece, notes if piece == 0 else out_maps), far)
+        waited = far
+        near, far = spread_piece(start_piece(piece, notes if piece == 0 else out_maps), far)
         run = functools.partial(accumulate, piece, step)
         shared = (gate_weight, up_weight, maps)
         if piece == 0:
-            *near_sums, near_label = run(True, near, near_sums, *shared, True, True, after=halves)
+            *near_sums, near_label = run(True, near, near_sums, *shared, True, True)
             *far_sums, far_label = run(False, far, far_sums, *shared, True, True)
         elif piece < PIECES - 1:
-            near_sums = run(True, near, near_sums, *shared, True, True, after=halves)
+            near_sums = run(True, near, near_sums, *shared, True, True)
             far_sums = run(False, far, far_sums, *shared, True, True)
         else:
-            near_sums = run(True, near, near_sums, *shared, True, True, after=halves)
+            near_sums = run(True, near, near_sums, *shared, True, True, after=waited)
             (far_low,) = run(False, far, far_sums[2:], *shared, False, True)
             far_acts = run(False, far, far_sums[:2], *shared, True, False)
     label_row = jnp.concatenate([near_label[:1], far_label[:1]], axis=1).astype(jnp.int32)

time: 315 us -> 301 us (0.956)
  local copies, waits for them, and re-layouts: 28.3 us -> 17.9 us
  waiting for transfers between devices: 148 us -> 144 us
    unnamed x97 -> x75, local copies, waits for them, and re-layouts: 24.6 us -> 16 us
    ppermute x22, waiting for transfers between devices: 72.3 us -> 68.2 us  [over_dp(): lax.ppermute(value, 'dp', [(i, (i + shift) % size) for i in range(size)])]
  transfers between devices with their start and end apart: 29 -> 29, of which waited for: 13 -> 15; matrix products, arithmetic and copies ran while one was open for 3% -> 2% of each run, Pallas kernels for 10% -> 12%
where the time goes in v2:
time: 301 us; the launch traced here: 300 us
  waiting for transfers between devices  144 us (48%)
  starting transfers between devices  78.7 us (26%)
  Pallas kernels  49.1 us (16%)
  local copies, waits for them, and re-layouts  17.9 us (6%)
  other arithmetic  8.65 us (3%)
    all_to_all x4, waiting for transfers between devices, exchange(): lax.all_to_all(rows, 'expert', split_axis=0, concat_axis=0, axis_index_gr...  73.6 us
    ppermute x22, waiting for transfers between devices, over_dp(): lax.ppermute(value, 'dp', [(i, (i + shift) % size) for i in range(size)])  68.2 us
    all_to_all x4, starting transfers between devices, exchange(): lax.all_to_all(rows, 'expert', split_axis=0, concat_axis=0, axis_index_gr...  45 us
    ppermute x22, starting transfers between devices, over_dp(): lax.ppermute(value, 'dp', [(i, (i + shift) % size) for i in range(size)])  28.8 us
    pallas_call x5, Pallas kernels, accumulate(): pl.pallas_call(functools.partial(accumulate_kernel, first, near, with_act...  17.7 us
    unnamed x75, local copies, waits for them, and re-layouts  16 us
    pallas_call x2, Pallas kernels, pass_blocks(): pl.pallas_call(pass_kernel, grid=(2, step // TILE), in_specs=[whole, whol...  7.71 us
    pallas_call x2, Pallas kernels, last_block(): pl.pallas_call(last_kernel, grid=(2, step // TILE), in_specs=[pl.BlockSpe...  6.79 us
  transfers between devices with their start and end apart: 29, of which 15 were waited for; matrix products, arithmetic and copies ran while one was open for 2% of the time, Pallas kernels for 12%

profile of v2, /device:TPU:1, one launch (start us, length us, event | category | flops | bytes accessed | tf_op | source)
XLA Modules:
  0.0 300.2 jit_solution(16238568670218257894)
XLA Ops:
  2.5 3.3 %collective-permute-start = (bf16[16,2176]{1,0:T(8,128)(2,1)S(1)}, bf16[16,2176]{1,0:T(8,128)(2,1)S(1)}, u32[]{:S(2)}, u32[]{:S(2)}) collective-permute-start(bf16[16,2176]{1,0:T(8,128)(2,1)S(1)} %concatenate.65), channel_id=1, source_target_pairs={{0,4},{4,0},{8,12},{12,8},{16,20},{20,16},{24,28},{28,24},{32,36},... | collective-permute-start | bytes 208904 | tf_op jit(solution)/shard_map/ppermute | solution.py:25
  9.5 2.4 shard_map.100
  12.0 10.3 %all-to-all-start = ((bf16[64,8,1152]{2,1,0:T(8,128)(2,1)}), bf16[64,8,1152]{2,1,0:T(8,128)(2,1)S(1)}, u32[]{:S(2)}, u32[]{:S(2)}) async-start(bf16[64,8,1152]{2,1,0:T(8,128)(2,1)} %bitcast.69), calls=%async_computation | async-start | bytes 2359296 | tf_op jit(solution)/shard_map/all_to_all | solution.py:33
  22.4 3.0 collective-permute-start.8
  26.9 1.1 collective-permute-done.8
  28.1 2.4 collective-permute-done.7
  32.0 2.3 shard_map.102
  34.3 20.0 %all-to-all-done = bf16[64,8,1152]{2,1,0:T(8,128)(2,1)S(1)} async-done(((bf16[64,8,1152]{2,1,0:T(8,128)(2,1)}), bf16[64,8,1152]{2,1,0:T(8,128)(2,1)S(1)}, u32[]{:S(2)}, u32[]{:S(2)}) %all-to-all-start) | async-done | bytes 1179680 | tf_op jit(solution)/shard_map/all_to_all | solution.py:33
  54.3 6.4 %all-to-all-start.1 = ((bf16[64,8,1024]{2,1,0:T(8,128)(2,1)}), bf16[64,8,1024]{2,1,0:T(8,128)(2,1)}, u32[]{:S(2)}, u32[]{:S(2)}) async-start(bf16[64,8,1024]{2,1,0:T(8,128)(2,1)} %bitcast.72), calls=%async_computation.1 | async-start | bytes 2097152 | tf_op jit(solution)/shard_map/all_to_all | solution.py:33
  60.7 1.4 collective-permute-start.2
  62.0 1.5 collective-permute-start.3
  63.6 26.6 %all-to-all-done.1 = bf16[64,8,1024]{2,1,0:T(8,128)(2,1)} async-done(((bf16[64,8,1024]{2,1,0:T(8,128)(2,1)}), bf16[64,8,1024]{2,1,0:T(8,128)(2,1)}, u32[]{:S(2)}, u32[]{:S(2)}) %all-to-all-start.1) | async-done | bytes 1048608 | tf_op jit(solution)/shard_map/all_to_all | solution.py:33
  90.2 1.3 collective-permute-start.9
  91.5 1.4 collective-permute-start.10
  92.9 1.4 fusion.25
  95.9 2.5 shard_map.101
  98.4 2.7 collective-permute-start.5
  102.1 13.3 %collective-permute-done.9.refs_3_.left = bf16[2,256,1024]{2,1,0:T(8,128)(2,1)} collective-permute-done((bf16[2,256,1024]{2,1,0:T(8,128)(2,1)}, bf16[2,256,1024]{2,1,0:T(8,128)(2,1)}, u32[]{:S(2)}, u32[]{:S(2)}) %collective-permute-start.9) | collective-permute-done | bytes 1048608 | tf_op jit(solution)/shard_map/ppermute | solution.py:20
  115.4 2.2 shard_map.106
  118.6 1.7 collective-permute-start.12
  120.3 1.9 copy-done.1
  122.2 1.2 copy-done.3
  123.4 1.3 copy-done.5
  124.7 1.3 copy-done.7
  126.0 6.1 %shard_map.103 = (f32[768,384]{1,0:T(8,128)S(1)}, f32[768,384]{1,0:T(8,128)S(1)}, f32[128,768]{1,0:T(8,128)S(1)}, f32[8,768]{1,0:T(8,128)S(1)}) custom-call(bf16[2,256,1152]{2,1,0:T(8,128)(2,1)S(1)} %bitcast.63, bf16[2,256,1152]{2,1,0:T(8,128)(2,1)S(1)} %copy-done.7, bf16[2,256,1152]{2,1,0:T(8,128)(2,1)} %collective-permute-done.3.right.refs_2_.refs_8_, ...), custom_call_target="tpu_custom_call" | custom-call | flops 2818572288 | bytes 8699904 | tf_op jit(solution)/shard_map/pallas_call | solution.py:129
  132.1 3.1 %shard_map.105 = (f32[256,384]{1,0:T(8,128)S(1)}, f32[256,384]{1,0:T(8,128)S(1)}, f32[128,256]{1,0:T(8,128)S(1)}, f32[8,256]{1,0:T(8,128)S(1)}) custom-call(bf16[1,256,1152]{2,1,0:T(8,128)(2,1)} %collective-permute-done.4.refs_0_.refs_5_, bf16[1,256,1152]{2,1,0:T(8,128)(2,1)} %collective-permute-done.5.refs_1_, bf16[1,4096,384]{2,1,0:T(8,128)(2,1)S(1)} %copy-done, ...), custom_call_target="tpu_custom_call" | custom-call | flops 939524096 | bytes 2899968 | tf_op jit(solution)/shard_map/pallas_call | solution.py:129
  135.2 6.2 %shard_map.104 = (f32[768,384]{1,0:T(8,128)S(1)}, f32[768,384]{1,0:T(8,128)S(1)}, f32[128,768]{1,0:T(8,128)S(1)}) custom-call(bf16[1,256,1152]{2,1,0:T(8,128)(2,1)} %collective-permute-done.4.refs_0_.refs_5_, bf16[1,256,1152]{2,1,0:T(8,128)(2,1)} %collective-permute-done.5.refs_1_, ...), custom_call_target="tpu_custom_call", output_to_operand_aliasing={{0}: (8, {}), {1}: (9, {}), {2}: (10, {})} | custom-call | flops 2818572288 | bytes 8650752 | tf_op jit(solution)/shard_map/pallas_call | solution.py:129
  143.9 1.2 collective-permute-start.15
  145.0 1.1 collective-permute-start.14
  146.6 1.5 shard_map.109
  148.6 1.8 collective-permute-done.13
  151.6 3.3 %shard_map.111 = (bf16[256,1024]{1,0:T(8,128)(2,1)}, bf16[256,1024]{1,0:T(8,128)(2,1)}) custom-call(bf16[256,384]{1,0:T(8,128)(2,1)} %copy-done.14, bf16[1,384,4096]{2,1,0:T(8,128)(2,1)} %weight.11), custom_call_target="tpu_custom_call" | custom-call | flops 402653184 | bytes 3145728 | tf_op jit(solution)/shard_map/pallas_call | solution.py:255
  154.9 2.7 collective-permute-start.17
  160.4 3.9 %collective-permute-done.16.lower = bf16[256,1024]{1,0:T(8,128)(2,1)S(1)} collective-permute-done((bf16[256,1024]{1,0:T(8,128)(2,1)}, bf16[256,1024]{1,0:T(8,128)(2,1)S(1)}, u32[]{:S(2)}, u32[]{:S(2)}) %collective-permute-start.16) | collective-permute-done | bytes 524320 | tf_op jit(solution)/shard_map/ppermute | solution.py:20
  165.1 3.8 %shard_map.112 = (bf16[2,256,1024]{2,1,0:T(8,128)(2,1)}, bf16[2,256,1024]{2,1,0:T(8,128)(2,1)}) custom-call(bf16[256,384]{1,0:T(8,128)(2,1)} %copy-done.16, bf16[256,384]{1,0:T(8,128)(2,1)} %copy-done.15, bf16[1,384,4096]{2,1,0:T(8,128)(2,1)} %weight.11, bf16[256,1024]{1,0:T(8,128)(2,1)} %copy-done.26, bf16[256,1024]{1,0:T(8,128)(2,1)} %collective-permute-done.17.upper), custom_call_target="tpu_custom_call" | custom-call | flops 805306368 | bytes 4718592 | tf_op jit(solution)/shard_map/pallas_call | solution.py:286
  169.0 2.7 collective-permute-start.19
  171.6 3.1 %shard_map.113 = (bf16[256,1024]{1,0:T(8,128)(2,1)}, bf16[256,1024]{1,0:T(8,128)(2,1)}) custom-call(bf16[256,384]{1,0:T(8,128)(2,1)} %copy-done.14, bf16[1,384,4096]{2,1,0:T(8,128)(2,1)} %weight.11), custom_call_target="tpu_custom_call" | custom-call | flops 402653184 | bytes 3145728 | tf_op jit(solution)/shard_map/pallas_call | solution.py:255
  174.8 2.7 collective-permute-start.21
  177.5 21.3 %collective-permute-done.20.refs_0_.lower = bf16[256,1024]{1,0:T(8,128)(2,1)S(1)} collective-permute-done((bf16[256,1024]{1,0:T(8,128)(2,1)}, bf16[256,1024]{1,0:T(8,128)(2,1)S(1)}, u32[]{:S(2)}, u32[]{:S(2)}) %collective-permute-start.20) | collective-permute-done | bytes 524320 | tf_op jit(solution)/shard_map/ppermute | solution.py:20
  200.4 3.4 %shard_map.114 = bf16[2,256,1024]{2,1,0:T(8,128)(2,1)} custom-call(bf16[256,384]{1,0:T(8,128)(2,1)} %copy-done.17, bf16[1,384,4096]{2,1,0:T(8,128)(2,1)} %weight.11, bf16[2,256,1024]{2,1,0:T(8,128)(2,1)} %copy-done.20, bf16[2,256,1024]{2,1,0:T(8,128)(2,1)} %copy-done.21, bf16[256,1024]{1,0:T(8,128)(2,1)} %copy-done.18, bf16[256,1024]{1,0:T(8,128)(2,1)} %copy-done.19), custom_call_target="tpu_custom_call" | custom-call | flops 402653184 | bytes 3145728 | tf_op jit(solution)/shard_map/pallas_call | solution.py:304
  203.7 17.1 %all-to-all-start.2 = ((bf16[64,8,1024]{2,1,0:T(8,128)(2,1)}), bf16[64,8,1024]{2,1,0:T(8,128)(2,1)S(1)}, u32[]{:S(2)}, u32[]{:S(2)}) async-start(bf16[64,8,1024]{2,1,0:T(8,128)(2,1)} %bitcast.70), calls=%async_computation.2 | async-start | bytes 2097152 | tf_op jit(solution)/shard_map/all_to_all | solution.py:33
  220.9 3.9 %shard_map.115 = (bf16[2,256,1024]{2,1,0:T(8,128)(2,1)}, bf16[2,256,1024]{2,1,0:T(8,128)(2,1)}) custom-call(bf16[256,384]{1,0:T(8,128)(2,1)} %copy-done.16, bf16[256,384]{1,0:T(8,128)(2,1)} %copy-done.15, bf16[1,384,4096]{2,1,0:T(8,128)(2,1)} %weight.11, bf16[256,1024]{1,0:T(8,128)(2,1)} %copy-done.18, bf16[256,1024]{1,0:T(8,128)(2,1)} %copy-done.19), custom_call_target="tpu_custom_call" | custom-call | flops 805306368 | bytes 4718592 | tf_op jit(solution)/shard_map/pallas_call | solution.py:286
  224.7 2.7 collective-permute-start.23
  227.4 23.1 %collective-permute-done.22.left = bf16[2,256,1024]{2,1,0:T(8,128)(2,1)S(1)} collective-permute-done((bf16[2,256,1024]{2,1,0:T(8,128)(2,1)}, bf16[2,256,1024]{2,1,0:T(8,128)(2,1)S(1)}, u32[]{:S(2)}, u32[]{:S(2)}) %collective-permute-start.22) | collective-permute-done | bytes 1048608 | tf_op jit(solution)/shard_map/ppermute | solution.py:20
  252.5 3.4 %shard_map.116 = bf16[2,256,1024]{2,1,0:T(8,128)(2,1)} custom-call(bf16[256,384]{1,0:T(8,128)(2,1)} %copy-done.17, bf16[1,384,4096]{2,1,0:T(8,128)(2,1)} %weight.11, bf16[2,256,1024]{2,1,0:T(8,128)(2,1)} %copy-done.22, bf16[2,256,1024]{2,1,0:T(8,128)(2,1)} %copy-done.23), custom_call_target="tpu_custom_call" | custom-call | flops 402653184 | bytes 3145728 | tf_op jit(solution)/shard_map/pallas_call | solution.py:304
  255.9 11.2 %all-to-all-start.3 = ((bf16[64,8,1024]{2,1,0:T(8,128)(2,1)}), bf16[64,8,1024]{2,1,0:T(8,128)(2,1)S(1)}, u32[]{:S(2)}, u32[]{:S(2)}) async-start(bf16[64,8,1024]{2,1,0:T(8,128)(2,1)} %bitcast.71), calls=%async_computation.3 | async-start | bytes 2097152 | tf_op jit(solution)/shard_map/all_to_all | solution.py:33
  269.7 27.0 %all-to-all-done.3 = bf16[64,8,1024]{2,1,0:T(8,128)(2,1)S(1)} async-done(((bf16[64,8,1024]{2,1,0:T(8,128)(2,1)}), bf16[64,8,1024]{2,1,0:T(8,128)(2,1)S(1)}, u32[]{:S(2)}, u32[]{:S(2)}) %all-to-all-start.3) | async-done | bytes 1048608 | tf_op jit(solution)/shard_map/all_to_all | solution.py:33
  297.5 1.1 collective-permute-start.24
  (155 shorter events, 29.4 us)
Async XLA Ops:
  2.5 4.2 %collective-permute-start = (bf16[16,2176]{1,0:T(8,128)(2,1)S(1)}, bf16[16,2176]{1,0:T(8,128)(2,1)S(1)}, u32[]{:S(2)}, u32[]{:S(2)}) collective-permute-start(bf16[16,2176]{1,0:T(8,128)(2,1)S(1)} %concatenate.65), channel_id=1, source_target_pairs={{0,4},{4,0},{8,12},{12,8},{16,20},{20,16},{24,28},{28,24},{32,36},... | collective-permute-start | bytes 208904 | tf_op jit(solution)/shard_map/ppermute | solution.py:25
  6.5 5.5 %copy-start.28 = (s32[512]{0:T(512)}, s32[512]{0:T(512)S(1)}, u32[]{:S(2)}) copy-start(s32[512]{0:T(512)S(1)} %eq.114) | copy-start | bytes 6148
  7.4 4.6 %copy-start.24 = (s32[64,32]{1,0:T(8,128)}, s32[64,32]{1,0:T(8,128)S(1)}, u32[]{:S(2)}) copy-start(s32[64,32]{1,0:T(8,128)S(1)} %copy.30) | copy-start | bytes 24580
  12.0 10.4 %copy-start.27 = (bf16[4,1,32,1536]{3,2,1,0:T(8,128)(2,1)S(1)}, bf16[4,1,32,1536]{3,2,1,0:T(8,128)(2,1)}, u32[]{:S(2)}) copy-start(bf16[4,1,32,1536]{3,2,1,0:T(8,128)(2,1)} %param.19) | copy-start | bytes 1179652
  12.0 42.3 %all-to-all-start = ((bf16[64,8,1152]{2,1,0:T(8,128)(2,1)}), bf16[64,8,1152]{2,1,0:T(8,128)(2,1)S(1)}, u32[]{:S(2)}, u32[]{:S(2)}) async-start(bf16[64,8,1152]{2,1,0:T(8,128)(2,1)} %bitcast.69), calls=%async_computation | async-start | bytes 2359296 | tf_op jit(solution)/shard_map/all_to_all | solution.py:33
  22.4 5.6 %collective-permute-start.8 = (bf16[4,32,384]{2,1,0:T(8,128)(2,1)S(1)}, bf16[4,32,384]{2,1,0:T(8,128)(2,1)S(1)}, u32[]{:S(2)}, u32[]{:S(2)}) collective-permute-start(bf16[4,32,384]{2,1,0:T(8,128)(2,1)S(1)} %get-tuple-element.65), channel_id=1, source_target_pairs={{0,2},{1,3},{2,0},{3,1},{4,6},{5,7},{6,4},{7,5},{8,10},{9,11},{10,... | collective-permute-start | bytes 294920 | tf_op jit(solution)/shard_map/ppermute | solution.py:20
  25.4 5.1 %collective-permute-start.7 = (bf16[4,32,384]{2,1,0:T(8,128)(2,1)S(1)}, bf16[4,32,384]{2,1,0:T(8,128)(2,1)S(1)}, u32[]{:S(2)}, u32[]{:S(2)}) collective-permute-start(bf16[4,32,384]{2,1,0:T(8,128)(2,1)S(1)} %get-tuple-element.66), channel_id=1, source_target_pairs={{0,3},{1,0},{2,1},{3,2},{4,7},{5,4},{6,5},{7,6},{8,11},{9,8},{10,9... | collective-permute-start | bytes 294920 | tf_op jit(solution)/shard_map/ppermute | solution.py:20
  26.2 5.0 %collective-permute-start.6 = (bf16[4,32,384]{2,1,0:T(8,128)(2,1)S(1)}, bf16[4,32,384]{2,1,0:T(8,128)(2,1)S(1)}, u32[]{:S(2)}, u32[]{:S(2)}) collective-permute-start(bf16[4,32,384]{2,1,0:T(8,128)(2,1)S(1)} %get-tuple-element.64), channel_id=1, source_target_pairs={{0,1},{1,2},{2,3},{3,0},{4,5},{5,6},{6,7},{7,4},{8,9},{9,10},{10,1... | collective-permute-start | bytes 294920 | tf_op jit(solution)/shard_map/ppermute | solution.py:20
  54.2 40.6 %copy-start.4 = (bf16[64,8,1152]{2,1,0:T(8,128)(2,1)}, bf16[64,8,1152]{2,1,0:T(8,128)(2,1)S(1)}, u32[]{:S(2)}) copy-start(bf16[64,8,1152]{2,1,0:T(8,128)(2,1)S(1)} %all-to-all-done) | copy-start | bytes 3538948
  54.3 35.9 %all-to-all-start.1 = ((bf16[64,8,1024]{2,1,0:T(8,128)(2,1)}), bf16[64,8,1024]{2,1,0:T(8,128)(2,1)}, u32[]{:S(2)}, u32[]{:S(2)}) async-start(bf16[64,8,1024]{2,1,0:T(8,128)(2,1)} %bitcast.72), calls=%async_computation.1 | async-start | bytes 2097152 | tf_op jit(solution)/shard_map/all_to_all | solution.py:33
  60.7 34.2 %collective-permute-start.2 = (bf16[2,256,1152]{2,1,0:T(8,128)(2,1)S(1)}, bf16[2,256,1152]{2,1,0:T(8,128)(2,1)S(1)}, u32[]{:S(2)}, u32[]{:S(2)}) collective-permute-start(bf16[2,256,1152]{2,1,0:T(8,128)(2,1)S(1)} %bitcast.61), channel_id=1, source_target_pairs={{0,1},{1,2},{2,3},{3,0},{4,5},{5,6},{6,7},{7,4},{8,9},{9,10},{10,1... | collective-permute-start | bytes 3538952 | tf_op jit(solution)/shard_map/ppermute | solution.py:20
  62.0 33.9 %collective-permute-start.3 = (bf16[2,256,1152]{2,1,0:T(8,128)(2,1)S(1)}, bf16[2,256,1152]{2,1,0:T(8,128)(2,1)}, u32[]{:S(2)}, u32[]{:S(2)}) collective-permute-start(bf16[2,256,1152]{2,1,0:T(8,128)(2,1)S(1)} %bitcast.62), channel_id=1, source_target_pairs={{0,3},{1,0},{2,1},{3,2},{4,7},{5,4},{6,5},{7,6},{8,11},{9,8},{10,9... | collective-permute-start | bytes 3538952 | tf_op jit(solution)/shard_map/ppermute | solution.py:20
  90.2 25.3 %collective-permute-start.9 = (bf16[2,256,1024]{2,1,0:T(8,128)(2,1)}, bf16[2,256,1024]{2,1,0:T(8,128)(2,1)}, u32[]{:S(2)}, u32[]{:S(2)}) collective-permute-start(bf16[2,256,1024]{2,1,0:T(8,128)(2,1)} %bitcast.12.refs_2_), channel_id=1, source_target_pairs={{0,1},{1,2},{2,3},{3,0},{4,5},{5,6},{6,7},{7,4},{8,9},{9,10},{10,1... | collective-permute-start | bytes 3145736 | tf_op jit(solution)/shard_map/ppermute | solution.py:20
  91.5 24.0 %collective-permute-start.10 = (bf16[2,256,1024]{2,1,0:T(8,128)(2,1)}, bf16[2,256,1024]{2,1,0:T(8,128)(2,1)}, u32[]{:S(2)}, u32[]{:S(2)}) collective-permute-start(bf16[2,256,1024]{2,1,0:T(8,128)(2,1)} %bitcast.12.refs_2_), channel_id=1, source_target_pairs={{0,3},{1,0},{2,1},{3,2},{4,7},{5,4},{6,5},{7,6},{8,11},{9,8},{10,9... | collective-permute-start | bytes 3145736 | tf_op jit(solution)/shard_map/ppermute | solution.py:20
  95.9 24.4 %copy-start = (bf16[1,4096,384]{2,1,0:T(8,128)(2,1)S(1)}, bf16[1,4096,384]{2,1,0:T(8,128)(2,1)}, u32[]{:S(2)}) copy-start(bf16[1,4096,384]{2,1,0:T(8,128)(2,1)} %refs_2_.3) | copy-start | bytes 9437188
  98.4 33.7 %collective-permute-start.4 = (bf16[1,256,1152]{2,1,0:T(8,128)(2,1)}, bf16[1,256,1152]{2,1,0:T(8,128)(2,1)}, u32[]{:S(2)}, u32[]{:S(2)}) collective-permute-start(bf16[1,256,1152]{2,1,0:T(8,128)(2,1)} %get-tuple-element.33), channel_id=1, source_target_pairs={{0,1},{1,2},{2,3},{3,0},{4,5},{5,6},{6,7},{7,4},{8,9},{9,10},{10,1... | collective-permute-start | bytes 1769480 | tf_op jit(solution)/shard_map/ppermute | solution.py:20
  98.4 33.7 %collective-permute-start.5 = (bf16[1,256,1152]{2,1,0:T(8,128)(2,1)}, bf16[1,256,1152]{2,1,0:T(8,128)(2,1)}, u32[]{:S(2)}, u32[]{:S(2)}) collective-permute-start(bf16[1,256,1152]{2,1,0:T(8,128)(2,1)} %get-tuple-element.34), channel_id=1, source_target_pairs={{0,3},{1,0},{2,1},{3,2},{4,7},{5,4},{6,5},{7,6},{8,11},{9,8},{10,9... | collective-permute-start | bytes 1769480 | tf_op jit(solution)/shard_map/ppermute | solution.py:20
  117.6 23.8 %collective-permute-start.11 = (bf16[1,256,1024]{2,1,0:T(8,128)(2,1)}, bf16[1,256,1024]{2,1,0:T(8,128)(2,1)S(1)}, u32[]{:S(2)}, u32[]{:S(2)}) collective-permute-start(bf16[1,256,1024]{2,1,0:T(8,128)(2,1)} %get-tuple-element.43), channel_id=1, source_target_pairs={{0,1},{1,2},{2,3},{3,0},{4,5},{5,6},{6,7},{7,4},{8,9},{9,10},{10,1... | collective-permute-start | bytes 1572872 | tf_op jit(solution)/shard_map/ppermute | solution.py:20
  118.6 22.9 %collective-permute-start.12 = (bf16[1,256,1024]{2,1,0:T(8,128)(2,1)}, bf16[1,256,1024]{2,1,0:T(8,128)(2,1)S(1)}, u32[]{:S(2)}, u32[]{:S(2)}) collective-permute-start(bf16[1,256,1024]{2,1,0:T(8,128)(2,1)} %get-tuple-element.44), channel_id=1, source_target_pairs={{0,3},{1,0},{2,1},{3,2},{4,7},{5,4},{6,5},{7,6},{8,11},{9,8},{10,9... | collective-permute-start | bytes 1572872 | tf_op jit(solution)/shard_map/ppermute | solution.py:20
  120.3 1.9 copy-start.1
  126.0 6.1 %copy-start.2 = (bf16[1,4096,384]{2,1,0:T(8,128)(2,1)S(1)}, bf16[1,4096,384]{2,1,0:T(8,128)(2,1)}, u32[]{:S(2)}) copy-start(bf16[1,4096,384]{2,1,0:T(8,128)(2,1)} %refs_3_.5) | copy-start | bytes 9437188
  141.5 2.2 copy-start.35
  141.5 2.2 copy-start.36
  143.6 3.0 copy-start.13
  143.9 4.7 %collective-permute-start.15 = (bf16[32,1024]{1,0:T(8,128)(2,1)S(1)}, bf16[32,1024]{1,0:T(8,128)(2,1)S(1)}, u32[]{:S(2)}, u32[]{:S(2)}) collective-permute-start(bf16[32,1024]{1,0:T(8,128)(2,1)S(1)} %get-tuple-element.74), channel_id=1, source_target_pairs={{0,2},{1,3},{2,0},{3,1},{4,6},{5,7},{6,4},{7,5},{8,10},{9,11},{10,... | collective-permute-start | bytes 196616 | tf_op jit(solution)/shard_map/ppermute | solution.py:20
  145.0 3.5 %collective-permute-start.14 = (bf16[32,1024]{1,0:T(8,128)(2,1)S(1)}, bf16[32,1024]{1,0:T(8,128)(2,1)S(1)}, u32[]{:S(2)}, u32[]{:S(2)}) collective-permute-start(bf16[32,1024]{1,0:T(8,128)(2,1)S(1)} %get-tuple-element.75), channel_id=1, source_target_pairs={{0,3},{1,0},{2,1},{3,2},{4,7},{5,4},{6,5},{7,6},{8,11},{9,8},{10,9... | collective-permute-start | bytes 196616 | tf_op jit(solution)/shard_map/ppermute | solution.py:20
  146.1 4.3 %collective-permute-start.13 = (bf16[32,1024]{1,0:T(8,128)(2,1)S(1)}, bf16[32,1024]{1,0:T(8,128)(2,1)S(1)}, u32[]{:S(2)}, u32[]{:S(2)}) collective-permute-start(bf16[32,1024]{1,0:T(8,128)(2,1)S(1)} %get-tuple-element.73), channel_id=1, source_target_pairs={{0,1},{1,2},{2,3},{3,0},{4,5},{5,6},{6,7},{7,4},{8,9},{9,10},{10,1... | collective-permute-start | bytes 196616 | tf_op jit(solution)/shard_map/ppermute | solution.py:20
  146.6 1.6 copy-start.30
  151.5 6.0 %copy-start.31 = (s32[1,1024]{1,0:T(1,128)S(1)}, s32[1,1024]{1,0:T(1,128)}, u32[]{:S(2)}) copy-start(s32[1,1024]{1,0:T(1,128)} %copy-done.30) | copy-start | bytes 12292
  151.5 6.0 %copy-start.9 = (f32[768,384]{1,0:T(8,128)S(1)}, f32[768,384]{1,0:T(8,128)}, u32[]{:S(2)}) copy-start(f32[768,384]{1,0:T(8,128)} %copy-done.8) | copy-start | bytes 3538948
  151.5 6.0 %copy-start.11 = (f32[768,384]{1,0:T(8,128)S(1)}, f32[768,384]{1,0:T(8,128)}, u32[]{:S(2)}) copy-start(f32[768,384]{1,0:T(8,128)} %copy-done.10) | copy-start | bytes 3538948
  154.9 9.5 %collective-permute-start.16 = (bf16[256,1024]{1,0:T(8,128)(2,1)}, bf16[256,1024]{1,0:T(8,128)(2,1)S(1)}, u32[]{:S(2)}, u32[]{:S(2)}) collective-permute-start(bf16[256,1024]{1,0:T(8,128)(2,1)} %get-tuple-element.53), channel_id=1, source_target_pairs={{0,1},{1,2},{2,3},{3,0},{4,5},{5,6},{6,7},{7,4},{8,9},{9,10},{10,1... | collective-permute-start | bytes 1572872 | tf_op jit(solution)/shard_map/ppermute | solution.py:20
  154.9 9.5 %collective-permute-start.17 = (bf16[256,1024]{1,0:T(8,128)(2,1)}, bf16[256,1024]{1,0:T(8,128)(2,1)}, u32[]{:S(2)}, u32[]{:S(2)}) collective-permute-start(bf16[256,1024]{1,0:T(8,128)(2,1)} %get-tuple-element.54), channel_id=1, source_target_pairs={{0,3},{1,0},{2,1},{3,2},{4,7},{5,4},{6,5},{7,6},{8,11},{9,8},{10,9... | collective-permute-start | bytes 1572872 | tf_op jit(solution)/shard_map/ppermute | solution.py:20
  169.0 29.8 %collective-permute-start.18 = (bf16[2,256,1024]{2,1,0:T(8,128)(2,1)}, bf16[2,256,1024]{2,1,0:T(8,128)(2,1)S(1)}, u32[]{:S(2)}, u32[]{:S(2)}) collective-permute-start(bf16[2,256,1024]{2,1,0:T(8,128)(2,1)} %get-tuple-element.55), channel_id=1, source_target_pairs={{0,1},{1,2},{2,3},{3,0},{4,5},{5,6},{6,7},{7,4},{8,9},{9,10},{10,1... | collective-permute-start | bytes 3145736 | tf_op jit(solution)/shard_map/ppermute | solution.py:20
  169.0 29.8 %collective-permute-start.19 = (bf16[2,256,1024]{2,1,0:T(8,128)(2,1)}, bf16[2,256,1024]{2,1,0:T(8,128)(2,1)S(1)}, u32[]{:S(2)}, u32[]{:S(2)}) collective-permute-start(bf16[2,256,1024]{2,1,0:T(8,128)(2,1)} %get-tuple-element.56), channel_id=1, source_target_pairs={{0,3},{1,0},{2,1},{3,2},{4,7},{5,4},{6,5},{7,6},{8,11},{9,8},{10,9... | collective-permute-start | bytes 3145736 | tf_op jit(solution)/shard_map/ppermute | solution.py:20
  174.8 23.9 %collective-permute-start.20 = (bf16[256,1024]{1,0:T(8,128)(2,1)}, bf16[256,1024]{1,0:T(8,128)(2,1)S(1)}, u32[]{:S(2)}, u32[]{:S(2)}) collective-permute-start(bf16[256,1024]{1,0:T(8,128)(2,1)} %get-tuple-element.57), channel_id=1, source_target_pairs={{0,1},{1,2},{2,3},{3,0},{4,5},{5,6},{6,7},{7,4},{8,9},{9,10},{10,1... | collective-permute-start | bytes 1572872 | tf_op jit(solution)/shard_map/ppermute | solution.py:20
  174.8 23.9 %collective-permute-start.21 = (bf16[256,1024]{1,0:T(8,128)(2,1)}, bf16[256,1024]{1,0:T(8,128)(2,1)S(1)}, u32[]{:S(2)}, u32[]{:S(2)}) collective-permute-start(bf16[256,1024]{1,0:T(8,128)(2,1)} %get-tuple-element.58), channel_id=1, source_target_pairs={{0,3},{1,0},{2,1},{3,2},{4,7},{5,4},{6,5},{7,6},{8,11},{9,8},{10,9... | collective-permute-start | bytes 1572872 | tf_op jit(solution)/shard_map/ppermute | solution.py:20
  198.8 1.6 copy-start.21
  203.7 52.2 %all-to-all-start.2 = ((bf16[64,8,1024]{2,1,0:T(8,128)(2,1)}), bf16[64,8,1024]{2,1,0:T(8,128)(2,1)S(1)}, u32[]{:S(2)}, u32[]{:S(2)}) async-start(bf16[64,8,1024]{2,1,0:T(8,128)(2,1)} %bitcast.70), calls=%async_computation.2 | async-start | bytes 2097152 | tf_op jit(solution)/shard_map/all_to_all | solution.py:33
  224.7 25.8 %collective-permute-start.22 = (bf16[2,256,1024]{2,1,0:T(8,128)(2,1)}, bf16[2,256,1024]{2,1,0:T(8,128)(2,1)S(1)}, u32[]{:S(2)}, u32[]{:S(2)}) collective-permute-start(bf16[2,256,1024]{2,1,0:T(8,128)(2,1)} %get-tuple-element.59), channel_id=1, source_target_pairs={{0,1},{1,2},{2,3},{3,0},{4,5},{5,6},{6,7},{7,4},{8,9},{9,10},{10,1... | collective-permute-start | bytes 3145736 | tf_op jit(solution)/shard_map/ppermute | solution.py:20
  224.7 25.8 %collective-permute-start.23 = (bf16[2,256,1024]{2,1,0:T(8,128)(2,1)}, bf16[2,256,1024]{2,1,0:T(8,128)(2,1)S(1)}, u32[]{:S(2)}, u32[]{:S(2)}) collective-permute-start(bf16[2,256,1024]{2,1,0:T(8,128)(2,1)} %get-tuple-element.60), channel_id=1, source_target_pairs={{0,3},{1,0},{2,1},{3,2},{4,7},{5,4},{6,5},{7,6},{8,11},{9,8},{10,9... | collective-permute-start | bytes 3145736 | tf_op jit(solution)/shard_map/ppermute | solution.py:20
  255.9 11.2 %copy-start.32 = (f32[16,8]{0,1:T(8,128)S(1)}, f32[16,8]{0,1:T(8,128)}, u32[]{:S(2)}) copy-start(f32[16,8]{0,1:T(8,128)} %param.12) | copy-start | bytes 1540
  255.9 12.7 %copy-start.34 = (s32[64]{0:T(128)S(1)}, s32[64]{0:T(128)}, u32[]{:S(2)}) copy-start(s32[64]{0:T(128)} %copy-done.33) | copy-start | bytes 772
  255.9 12.9 %copy-start.25 = (s32[64,32]{1,0:T(8,128)S(1)}, s32[64,32]{1,0:T(8,128)}, u32[]{:S(2)}) copy-start(s32[64,32]{1,0:T(8,128)} %copy-done.24) | copy-start | bytes 24580
  255.9 12.9 %copy-start.29 = (s32[512]{0:T(512)S(1)}, s32[512]{0:T(512)}, u32[]{:S(2)}) copy-start(s32[512]{0:T(512)} %copy-done.28) | copy-start | bytes 6148
  255.9 40.8 %all-to-all-start.3 = ((bf16[64,8,1024]{2,1,0:T(8,128)(2,1)}), bf16[64,8,1024]{2,1,0:T(8,128)(2,1)S(1)}, u32[]{:S(2)}, u32[]{:S(2)}) async-start(bf16[64,8,1024]{2,1,0:T(8,128)(2,1)} %bitcast.71), calls=%async_computation.3 | async-start | bytes 2097152 | tf_op jit(solution)/shard_map/all_to_all | solution.py:33
  267.2 1.3 collective-permute-start.1
  297.5 2.0 collective-permute-start.24
  (18 other events, 17.1 us)

commit v3 on v2

--- a/solution.py
+++ b/solution.py
@@ -134,7 +134,7 @@
         out_shape=tuple(jax.ShapeDtypeStruct(shape, F32) for shape in shapes),
         input_output_aliases=aliases,
         cost_estimate=pl.CostEstimate(flops=flops, bytes_accessed=moved, transcendentals=0),
-        compiler_params=pltpu.CompilerParams(vmem_limit_bytes=40 * 2**20),
+        compiler_params=pltpu.CompilerParams(vmem_limit_bytes=24 * 2**20),
     )(*operands)
 
 
@@ -173,7 +173,7 @@
         cost_estimate=pl.CostEstimate(
             flops=4 * total * hid * gate_b.shape[0], bytes_accessed=9 * total * hid, transcendentals=total * hid
         ),
-        compiler_params=pltpu.CompilerParams(vmem_limit_bytes=40 * 2**20),
+        compiler_params=pltpu.CompilerParams(vmem_limit_bytes=24 * 2**20),
     )(gate, up, low, tenants, gate_b, up_b)
 
 

time: 301 us -> 300 us (level)
    unnamed x75 -> x73, local copies, waits for them, and re-layouts: 16 us -> 15.7 us
  transfers between devices with their start and end apart: 29 -> 29, of which waited for: 15 -> 14; matrix products, arithmetic and copies ran while one was open for 2% -> 2% of each run, Pallas kernels for 12% -> 12%
where the time goes in v3:
time: 300 us; the launch traced here: 299 us
  waiting for transfers between devices  143 us (48%)
  starting transfers between devices  78.6 us (26%)
  Pallas kernels  49.1 us (16%)
  local copies, waits for them, and re-layouts  17.7 us (6%)
  other arithmetic  8.62 us (3%)
    all_to_all x4, waiting for transfers between devices, exchange(): lax.all_to_all(rows, 'expert', split_axis=0, concat_axis=0, axis_index_gr...  73.6 us
    ppermute x22, waiting for transfers between devices, over_dp(): lax.ppermute(value, 'dp', [(i, (i + shift) % size) for i in range(size)])  67.7 us
    all_to_all x4, starting transfers between devices, exchange(): lax.all_to_all(rows, 'expert', split_axis=0, concat_axis=0, axis_index_gr...  45 us
    ppermute x22, starting transfers between devices, over_dp(): lax.ppermute(value, 'dp', [(i, (i + shift) % size) for i in range(size)])  28.8 us
    pallas_call x5, Pallas kernels, accumulate(): pl.pallas_call(functools.partial(accumulate_kernel, first, near, with_act...  17.6 us
    unnamed x73, local copies, waits for them, and re-layouts  15.7 us
    pallas_call x2, Pallas kernels, pass_blocks(): pl.pallas_call(pass_kernel, grid=(2, step // TILE), in_specs=[whole, whol...  7.68 us
    pallas_call x2, Pallas kernels, last_block(): pl.pallas_call(last_kernel, grid=(2, step // TILE), in_specs=[pl.BlockSpe...  6.81 us
  transfers between devices with their start and end apart: 29, of which 14 were waited for; matrix products, arithmetic and copies ran while one was open for 2% of the time, Pallas kernels for 12%

profile of v3, /device:TPU:1, one launch (start us, length us, event | category | flops | bytes accessed | tf_op | source)
XLA Modules:
  0.0 299.4 jit_solution(3379929953955784306)
XLA Ops:
  2.5 3.3 %collective-permute-start = (bf16[16,2176]{1,0:T(8,128)(2,1)S(1)}, bf16[16,2176]{1,0:T(8,128)(2,1)S(1)}, u32[]{:S(2)}, u32[]{:S(2)}) collective-permute-start(bf16[16,2176]{1,0:T(8,128)(2,1)S(1)} %concatenate.65), channel_id=1, source_target_pairs={{0,4},{4,0},{8,12},{12,8},{16,20},{20,16},{24,28},{28,24},{32,36},... | collective-permute-start | bytes 208904 | tf_op jit(solution)/shard_map/ppermute | solution.py:25
  9.5 2.4 shard_map.100
  12.0 10.3 %all-to-all-start = ((bf16[64,8,1152]{2,1,0:T(8,128)(2,1)}), bf16[64,8,1152]{2,1,0:T(8,128)(2,1)S(1)}, u32[]{:S(2)}, u32[]{:S(2)}) async-start(bf16[64,8,1152]{2,1,0:T(8,128)(2,1)} %bitcast.69), calls=%async_computation | async-start | bytes 2359296 | tf_op jit(solution)/shard_map/all_to_all | solution.py:33
  22.5 3.0 collective-permute-start.8
  26.9 1.2 collective-permute-done.8
  28.1 2.4 collective-permute-done.7
  32.0 2.3 shard_map.102
  34.3 20.0 %all-to-all-done = bf16[64,8,1152]{2,1,0:T(8,128)(2,1)S(1)} async-done(((bf16[64,8,1152]{2,1,0:T(8,128)(2,1)}), bf16[64,8,1152]{2,1,0:T(8,128)(2,1)S(1)}, u32[]{:S(2)}, u32[]{:S(2)}) %all-to-all-start) | async-done | bytes 1179680 | tf_op jit(solution)/shard_map/all_to_all | solution.py:33
  54.3 6.4 %all-to-all-start.1 = ((bf16[64,8,1024]{2,1,0:T(8,128)(2,1)}), bf16[64,8,1024]{2,1,0:T(8,128)(2,1)}, u32[]{:S(2)}, u32[]{:S(2)}) async-start(bf16[64,8,1024]{2,1,0:T(8,128)(2,1)} %bitcast.72), calls=%async_computation.1 | async-start | bytes 2097152 | tf_op jit(solution)/shard_map/all_to_all | solution.py:33
  60.7 1.4 collective-permute-start.2
  62.0 1.5 collective-permute-start.3
  63.6 26.6 %all-to-all-done.1 = bf16[64,8,1024]{2,1,0:T(8,128)(2,1)} async-done(((bf16[64,8,1024]{2,1,0:T(8,128)(2,1)}), bf16[64,8,1024]{2,1,0:T(8,128)(2,1)}, u32[]{:S(2)}, u32[]{:S(2)}) %all-to-all-start.1) | async-done | bytes 1048608 | tf_op jit(solution)/shard_map/all_to_all | solution.py:33
  90.2 1.3 collective-permute-start.9
  91.5 1.4 collective-permute-start.10
  92.9 1.4 fusion.25
  95.9 2.5 shard_map.101
  98.4 2.7 collective-permute-start.5
  102.1 13.3 %collective-permute-done.9.refs_3_.left = bf16[2,256,1024]{2,1,0:T(8,128)(2,1)} collective-permute-done((bf16[2,256,1024]{2,1,0:T(8,128)(2,1)}, bf16[2,256,1024]{2,1,0:T(8,128)(2,1)}, u32[]{:S(2)}, u32[]{:S(2)}) %collective-permute-start.9) | collective-permute-done | bytes 1048608 | tf_op jit(solution)/shard_map/ppermute | solution.py:20
  115.4 2.2 shard_map.106
  118.6 1.7 collective-permute-start.12
  120.3 1.9 copy-done.1
  122.2 1.2 copy-done.3
  123.4 1.3 copy-done.6
  124.7 1.3 copy-done.8
  126.0 6.1 %shard_map.103 = (f32[768,384]{1,0:T(8,128)S(1)}, f32[768,384]{1,0:T(8,128)S(1)}, f32[128,768]{1,0:T(8,128)S(1)}, f32[8,768]{1,0:T(8,128)S(1)}) custom-call(bf16[2,256,1152]{2,1,0:T(8,128)(2,1)S(1)} %bitcast.63, bf16[2,256,1152]{2,1,0:T(8,128)(2,1)S(1)} %copy-done.8, bf16[2,256,1152]{2,1,0:T(8,128)(2,1)} %collective-permute-done.3.right.refs_2_.refs_8_, ...), custom_call_target="tpu_custom_call" | custom-call | flops 2818572288 | bytes 8699904 | tf_op jit(solution)/shard_map/pallas_call | solution.py:129
  132.1 3.1 %shard_map.105 = (f32[256,384]{1,0:T(8,128)S(1)}, f32[256,384]{1,0:T(8,128)S(1)}, f32[128,256]{1,0:T(8,128)S(1)}, f32[8,256]{1,0:T(8,128)S(1)}) custom-call(bf16[1,256,1152]{2,1,0:T(8,128)(2,1)} %collective-permute-done.4.refs_0_.refs_5_, bf16[1,256,1152]{2,1,0:T(8,128)(2,1)} %collective-permute-done.5.refs_1_, bf16[1,4096,384]{2,1,0:T(8,128)(2,1)S(1)} %copy-done, ...), custom_call_target="tpu_custom_call" | custom-call | flops 939524096 | bytes 2899968 | tf_op jit(solution)/shard_map/pallas_call | solution.py:129
  135.2 6.2 %shard_map.104 = (f32[768,384]{1,0:T(8,128)S(1)}, f32[768,384]{1,0:T(8,128)S(1)}, f32[128,768]{1,0:T(8,128)S(1)}) custom-call(bf16[1,256,1152]{2,1,0:T(8,128)(2,1)} %collective-permute-done.4.refs_0_.refs_5_, bf16[1,256,1152]{2,1,0:T(8,128)(2,1)} %collective-permute-done.5.refs_1_, ...), custom_call_target="tpu_custom_call", output_to_operand_aliasing={{0}: (8, {}), {1}: (9, {}), {2}: (10, {})} | custom-call | flops 2818572288 | bytes 8650752 | tf_op jit(solution)/shard_map/pallas_call | solution.py:129
  143.1 1.2 collective-permute-start.15
  144.3 1.1 collective-permute-start.14
  146.4 1.5 shard_map.109
  147.9 1.7 collective-permute-done.13
  150.8 3.3 %shard_map.111 = (bf16[256,1024]{1,0:T(8,128)(2,1)}, bf16[256,1024]{1,0:T(8,128)(2,1)}) custom-call(bf16[256,384]{1,0:T(8,128)(2,1)} %copy-done.13, bf16[1,384,4096]{2,1,0:T(8,128)(2,1)} %weight.11), custom_call_target="tpu_custom_call" | custom-call | flops 402653184 | bytes 3145728 | tf_op jit(solution)/shard_map/pallas_call | solution.py:255
  154.1 2.7 collective-permute-start.17
  159.6 3.9 %collective-permute-done.16.lower = bf16[256,1024]{1,0:T(8,128)(2,1)S(1)} collective-permute-done((bf16[256,1024]{1,0:T(8,128)(2,1)}, bf16[256,1024]{1,0:T(8,128)(2,1)S(1)}, u32[]{:S(2)}, u32[]{:S(2)}) %collective-permute-start.16) | collective-permute-done | bytes 524320 | tf_op jit(solution)/shard_map/ppermute | solution.py:20
  164.3 3.8 %shard_map.112 = (bf16[2,256,1024]{2,1,0:T(8,128)(2,1)}, bf16[2,256,1024]{2,1,0:T(8,128)(2,1)}) custom-call(bf16[256,384]{1,0:T(8,128)(2,1)} %copy-done.15, bf16[256,384]{1,0:T(8,128)(2,1)} %copy-done.14, bf16[1,384,4096]{2,1,0:T(8,128)(2,1)} %weight.11, bf16[256,1024]{1,0:T(8,128)(2,1)} %copy-done.25, bf16[256,1024]{1,0:T(8,128)(2,1)} %collective-permute-done.17.upper), custom_call_target="tpu_custom_call" | custom-call | flops 805306368 | bytes 4718592 | tf_op jit(solution)/shard_map/pallas_call | solution.py:286
  168.2 2.7 collective-permute-start.19
  170.8 3.1 %shard_map.113 = (bf16[256,1024]{1,0:T(8,128)(2,1)}, bf16[256,1024]{1,0:T(8,128)(2,1)}) custom-call(bf16[256,384]{1,0:T(8,128)(2,1)} %copy-done.13, bf16[1,384,4096]{2,1,0:T(8,128)(2,1)} %weight.11), custom_call_target="tpu_custom_call" | custom-call | flops 402653184 | bytes 3145728 | tf_op jit(solution)/shard_map/pallas_call | solution.py:255
  174.0 2.7 collective-permute-start.21
  176.6 21.3 %collective-permute-done.20.refs_0_.lower = bf16[256,1024]{1,0:T(8,128)(2,1)S(1)} collective-permute-done((bf16[256,1024]{1,0:T(8,128)(2,1)}, bf16[256,1024]{1,0:T(8,128)(2,1)S(1)}, u32[]{:S(2)}, u32[]{:S(2)}) %collective-permute-start.20) | collective-permute-done | bytes 524320 | tf_op jit(solution)/shard_map/ppermute | solution.py:20
  199.6 3.4 %shard_map.114 = bf16[2,256,1024]{2,1,0:T(8,128)(2,1)} custom-call(bf16[256,384]{1,0:T(8,128)(2,1)} %copy-done.16, bf16[1,384,4096]{2,1,0:T(8,128)(2,1)} %weight.11, bf16[2,256,1024]{2,1,0:T(8,128)(2,1)} %copy-done.19, bf16[2,256,1024]{2,1,0:T(8,128)(2,1)} %copy-done.20, bf16[256,1024]{1,0:T(8,128)(2,1)} %copy-done.17, bf16[256,1024]{1,0:T(8,128)(2,1)} %copy-done.18), custom_call_target="tpu_custom_call" | custom-call | flops 402653184 | bytes 3145728 | tf_op jit(solution)/shard_map/pallas_call | solution.py:304
  203.0 17.1 %all-to-all-start.2 = ((bf16[64,8,1024]{2,1,0:T(8,128)(2,1)}), bf16[64,8,1024]{2,1,0:T(8,128)(2,1)S(1)}, u32[]{:S(2)}, u32[]{:S(2)}) async-start(bf16[64,8,1024]{2,1,0:T(8,128)(2,1)} %bitcast.70), calls=%async_computation.2 | async-start | bytes 2097152 | tf_op jit(solution)/shard_map/all_to_all | solution.py:33
  220.1 3.9 %shard_map.115 = (bf16[2,256,1024]{2,1,0:T(8,128)(2,1)}, bf16[2,256,1024]{2,1,0:T(8,128)(2,1)}) custom-call(bf16[256,384]{1,0:T(8,128)(2,1)} %copy-done.15, bf16[256,384]{1,0:T(8,128)(2,1)} %copy-done.14, bf16[1,384,4096]{2,1,0:T(8,128)(2,1)} %weight.11, bf16[256,1024]{1,0:T(8,128)(2,1)} %copy-done.17, bf16[256,1024]{1,0:T(8,128)(2,1)} %copy-done.18), custom_call_target="tpu_custom_call" | custom-call | flops 805306368 | bytes 4718592 | tf_op jit(solution)/shard_map/pallas_call | solution.py:286
  223.9 2.7 collective-permute-start.23
  226.6 23.1 %collective-permute-done.22.left = bf16[2,256,1024]{2,1,0:T(8,128)(2,1)S(1)} collective-permute-done((bf16[2,256,1024]{2,1,0:T(8,128)(2,1)}, bf16[2,256,1024]{2,1,0:T(8,128)(2,1)S(1)}, u32[]{:S(2)}, u32[]{:S(2)}) %collective-permute-start.22) | collective-permute-done | bytes 1048608 | tf_op jit(solution)/shard_map/ppermute | solution.py:20
  251.7 3.4 %shard_map.116 = bf16[2,256,1024]{2,1,0:T(8,128)(2,1)} custom-call(bf16[256,384]{1,0:T(8,128)(2,1)} %copy-done.16, bf16[1,384,4096]{2,1,0:T(8,128)(2,1)} %weight.11, bf16[2,256,1024]{2,1,0:T(8,128)(2,1)} %copy-done.21, bf16[2,256,1024]{2,1,0:T(8,128)(2,1)} %copy-done.22), custom_call_target="tpu_custom_call" | custom-call | flops 402653184 | bytes 3145728 | tf_op jit(solution)/shard_map/pallas_call | solution.py:304
  255.2 11.2 %all-to-all-start.3 = ((bf16[64,8,1024]{2,1,0:T(8,128)(2,1)}), bf16[64,8,1024]{2,1,0:T(8,128)(2,1)S(1)}, u32[]{:S(2)}, u32[]{:S(2)}) async-start(bf16[64,8,1024]{2,1,0:T(8,128)(2,1)} %bitcast.71), calls=%async_computation.3 | async-start | bytes 2097152 | tf_op jit(solution)/shard_map/all_to_all | solution.py:33
  268.9 27.0 %all-to-all-done.3 = bf16[64,8,1024]{2,1,0:T(8,128)(2,1)S(1)} async-done(((bf16[64,8,1024]{2,1,0:T(8,128)(2,1)}), bf16[64,8,1024]{2,1,0:T(8,128)(2,1)S(1)}, u32[]{:S(2)}, u32[]{:S(2)}) %all-to-all-start.3) | async-done | bytes 1048608 | tf_op jit(solution)/shard_map/all_to_all | solution.py:33
  296.7 1.1 collective-permute-start.24
  (153 shorter events, 28.7 us)
Async XLA Ops:
  2.5 4.2 %collective-permute-start = (bf16[16,2176]{1,0:T(8,128)(2,1)S(1)}, bf16[16,2176]{1,0:T(8,128)(2,1)S(1)}, u32[]{:S(2)}, u32[]{:S(2)}) collective-permute-start(bf16[16,2176]{1,0:T(8,128)(2,1)S(1)} %concatenate.65), channel_id=1, source_target_pairs={{0,4},{4,0},{8,12},{12,8},{16,20},{20,16},{24,28},{28,24},{32,36},... | collective-permute-start | bytes 208904 | tf_op jit(solution)/shard_map/ppermute | solution.py:25
  6.5 5.4 %copy-start.27 = (s32[512]{0:T(512)}, s32[512]{0:T(512)S(1)}, u32[]{:S(2)}) copy-start(s32[512]{0:T(512)S(1)} %eq.114) | copy-start | bytes 6148
  7.4 4.6 %copy-start.23 = (s32[64,32]{1,0:T(8,128)}, s32[64,32]{1,0:T(8,128)S(1)}, u32[]{:S(2)}) copy-start(s32[64,32]{1,0:T(8,128)S(1)} %copy.30) | copy-start | bytes 24580
  12.0 10.4 %copy-start.26 = (bf16[4,1,32,1536]{3,2,1,0:T(8,128)(2,1)S(1)}, bf16[4,1,32,1536]{3,2,1,0:T(8,128)(2,1)}, u32[]{:S(2)}) copy-start(bf16[4,1,32,1536]{3,2,1,0:T(8,128)(2,1)} %param.19) | copy-start | bytes 1179652
  12.0 42.3 %all-to-all-start = ((bf16[64,8,1152]{2,1,0:T(8,128)(2,1)}), bf16[64,8,1152]{2,1,0:T(8,128)(2,1)S(1)}, u32[]{:S(2)}, u32[]{:S(2)}) async-start(bf16[64,8,1152]{2,1,0:T(8,128)(2,1)} %bitcast.69), calls=%async_computation | async-start | bytes 2359296 | tf_op jit(solution)/shard_map/all_to_all | solution.py:33
  22.5 5.6 %collective-permute-start.8 = (bf16[4,32,384]{2,1,0:T(8,128)(2,1)S(1)}, bf16[4,32,384]{2,1,0:T(8,128)(2,1)S(1)}, u32[]{:S(2)}, u32[]{:S(2)}) collective-permute-start(bf16[4,32,384]{2,1,0:T(8,128)(2,1)S(1)} %get-tuple-element.65), channel_id=1, source_target_pairs={{0,2},{1,3},{2,0},{3,1},{4,6},{5,7},{6,4},{7,5},{8,10},{9,11},{10,... | collective-permute-start | bytes 294920 | tf_op jit(solution)/shard_map/ppermute | solution.py:20
  25.4 5.1 %collective-permute-start.7 = (bf16[4,32,384]{2,1,0:T(8,128)(2,1)S(1)}, bf16[4,32,384]{2,1,0:T(8,128)(2,1)S(1)}, u32[]{:S(2)}, u32[]{:S(2)}) collective-permute-start(bf16[4,32,384]{2,1,0:T(8,128)(2,1)S(1)} %get-tuple-element.66), channel_id=1, source_target_pairs={{0,3},{1,0},{2,1},{3,2},{4,7},{5,4},{6,5},{7,6},{8,11},{9,8},{10,9... | collective-permute-start | bytes 294920 | tf_op jit(solution)/shard_map/ppermute | solution.py:20
  26.2 5.0 %collective-permute-start.6 = (bf16[4,32,384]{2,1,0:T(8,128)(2,1)S(1)}, bf16[4,32,384]{2,1,0:T(8,128)(2,1)S(1)}, u32[]{:S(2)}, u32[]{:S(2)}) collective-permute-start(bf16[4,32,384]{2,1,0:T(8,128)(2,1)S(1)} %get-tuple-element.64), channel_id=1, source_target_pairs={{0,1},{1,2},{2,3},{3,0},{4,5},{5,6},{6,7},{7,4},{8,9},{9,10},{10,1... | collective-permute-start | bytes 294920 | tf_op jit(solution)/shard_map/ppermute | solution.py:20
  54.3 40.6 %copy-start.5 = (bf16[64,8,1152]{2,1,0:T(8,128)(2,1)}, bf16[64,8,1152]{2,1,0:T(8,128)(2,1)S(1)}, u32[]{:S(2)}) copy-start(bf16[64,8,1152]{2,1,0:T(8,128)(2,1)S(1)} %all-to-all-done) | copy-start | bytes 3538948
  54.3 35.9 %all-to-all-start.1 = ((bf16[64,8,1024]{2,1,0:T(8,128)(2,1)}), bf16[64,8,1024]{2,1,0:T(8,128)(2,1)}, u32[]{:S(2)}, u32[]{:S(2)}) async-start(bf16[64,8,1024]{2,1,0:T(8,128)(2,1)} %bitcast.72), calls=%async_computation.1 | async-start | bytes 2097152 | tf_op jit(solution)/shard_map/all_to_all | solution.py:33
  60.7 34.2 %collective-permute-start.2 = (bf16[2,256,1152]{2,1,0:T(8,128)(2,1)S(1)}, bf16[2,256,1152]{2,1,0:T(8,128)(2,1)S(1)}, u32[]{:S(2)}, u32[]{:S(2)}) collective-permute-start(bf16[2,256,1152]{2,1,0:T(8,128)(2,1)S(1)} %bitcast.61), channel_id=1, source_target_pairs={{0,1},{1,2},{2,3},{3,0},{4,5},{5,6},{6,7},{7,4},{8,9},{9,10},{10,1... | collective-permute-start | bytes 3538952 | tf_op jit(solution)/shard_map/ppermute | solution.py:20
  62.0 33.8 %collective-permute-start.3 = (bf16[2,256,1152]{2,1,0:T(8,128)(2,1)S(1)}, bf16[2,256,1152]{2,1,0:T(8,128)(2,1)}, u32[]{:S(2)}, u32[]{:S(2)}) collective-permute-start(bf16[2,256,1152]{2,1,0:T(8,128)(2,1)S(1)} %bitcast.62), channel_id=1, source_target_pairs={{0,3},{1,0},{2,1},{3,2},{4,7},{5,4},{6,5},{7,6},{8,11},{9,8},{10,9... | collective-permute-start | bytes 3538952 | tf_op jit(solution)/shard_map/ppermute | solution.py:20
  90.2 25.2 %collective-permute-start.9 = (bf16[2,256,1024]{2,1,0:T(8,128)(2,1)}, bf16[2,256,1024]{2,1,0:T(8,128)(2,1)}, u32[]{:S(2)}, u32[]{:S(2)}) collective-permute-start(bf16[2,256,1024]{2,1,0:T(8,128)(2,1)} %bitcast.12.refs_2_), channel_id=1, source_target_pairs={{0,1},{1,2},{2,3},{3,0},{4,5},{5,6},{6,7},{7,4},{8,9},{9,10},{10,1... | collective-permute-start | bytes 3145736 | tf_op jit(solution)/shard_map/ppermute | solution.py:20
  91.5 24.0 %collective-permute-start.10 = (bf16[2,256,1024]{2,1,0:T(8,128)(2,1)}, bf16[2,256,1024]{2,1,0:T(8,128)(2,1)}, u32[]{:S(2)}, u32[]{:S(2)}) collective-permute-start(bf16[2,256,1024]{2,1,0:T(8,128)(2,1)} %bitcast.12.refs_2_), channel_id=1, source_target_pairs={{0,3},{1,0},{2,1},{3,2},{4,7},{5,4},{6,5},{7,6},{8,11},{9,8},{10,9... | collective-permute-start | bytes 3145736 | tf_op jit(solution)/shard_map/ppermute | solution.py:20
  95.9 24.4 %copy-start = (bf16[1,4096,384]{2,1,0:T(8,128)(2,1)S(1)}, bf16[1,4096,384]{2,1,0:T(8,128)(2,1)}, u32[]{:S(2)}) copy-start(bf16[1,4096,384]{2,1,0:T(8,128)(2,1)} %refs_2_.3) | copy-start | bytes 9437188
  98.3 33.7 %collective-permute-start.4 = (bf16[1,256,1152]{2,1,0:T(8,128)(2,1)}, bf16[1,256,1152]{2,1,0:T(8,128)(2,1)}, u32[]{:S(2)}, u32[]{:S(2)}) collective-permute-start(bf16[1,256,1152]{2,1,0:T(8,128)(2,1)} %get-tuple-element.33), channel_id=1, source_target_pairs={{0,1},{1,2},{2,3},{3,0},{4,5},{5,6},{6,7},{7,4},{8,9},{9,10},{10,1... | collective-permute-start | bytes 1769480 | tf_op jit(solution)/shard_map/ppermute | solution.py:20
  98.4 33.7 %collective-permute-start.5 = (bf16[1,256,1152]{2,1,0:T(8,128)(2,1)}, bf16[1,256,1152]{2,1,0:T(8,128)(2,1)}, u32[]{:S(2)}, u32[]{:S(2)}) collective-permute-start(bf16[1,256,1152]{2,1,0:T(8,128)(2,1)} %get-tuple-element.34), channel_id=1, source_target_pairs={{0,3},{1,0},{2,1},{3,2},{4,7},{5,4},{6,5},{7,6},{8,11},{9,8},{10,9... | collective-permute-start | bytes 1769480 | tf_op jit(solution)/shard_map/ppermute | solution.py:20
  117.6 23.8 %collective-permute-start.11 = (bf16[1,256,1024]{2,1,0:T(8,128)(2,1)}, bf16[1,256,1024]{2,1,0:T(8,128)(2,1)S(1)}, u32[]{:S(2)}, u32[]{:S(2)}) collective-permute-start(bf16[1,256,1024]{2,1,0:T(8,128)(2,1)} %get-tuple-element.43), channel_id=1, source_target_pairs={{0,1},{1,2},{2,3},{3,0},{4,5},{5,6},{6,7},{7,4},{8,9},{9,10},{10,1... | collective-permute-start | bytes 1572872 | tf_op jit(solution)/shard_map/ppermute | solution.py:20
  118.6 22.9 %collective-permute-start.12 = (bf16[1,256,1024]{2,1,0:T(8,128)(2,1)}, bf16[1,256,1024]{2,1,0:T(8,128)(2,1)S(1)}, u32[]{:S(2)}, u32[]{:S(2)}) collective-permute-start(bf16[1,256,1024]{2,1,0:T(8,128)(2,1)} %get-tuple-element.44), channel_id=1, source_target_pairs={{0,3},{1,0},{2,1},{3,2},{4,7},{5,4},{6,5},{7,6},{8,11},{9,8},{10,9... | collective-permute-start | bytes 1572872 | tf_op jit(solution)/shard_map/ppermute | solution.py:20
  120.3 1.9 copy-start.1
  126.0 6.1 %copy-start.2 = (bf16[1,4096,384]{2,1,0:T(8,128)(2,1)S(1)}, bf16[1,4096,384]{2,1,0:T(8,128)(2,1)}, u32[]{:S(2)}) copy-start(bf16[1,4096,384]{2,1,0:T(8,128)(2,1)} %refs_3_.5) | copy-start | bytes 9437188
  126.0 6.1 %copy-start.4 = (bf16[4,1,32,4096]{3,2,1,0:T(8,128)(2,1)S(1)}, bf16[4,1,32,4096]{3,2,1,0:T(8,128)(2,1)}, u32[]{:S(2)}) copy-start(bf16[4,1,32,4096]{3,2,1,0:T(8,128)(2,1)} %param.18) | copy-start | bytes 3145732
  141.4 1.4 copy-start.11
  141.5 1.4 copy-start.34
  141.5 1.4 copy-start.35
  143.1 4.8 %collective-permute-start.15 = (bf16[32,1024]{1,0:T(8,128)(2,1)S(1)}, bf16[32,1024]{1,0:T(8,128)(2,1)S(1)}, u32[]{:S(2)}, u32[]{:S(2)}) collective-permute-start(bf16[32,1024]{1,0:T(8,128)(2,1)S(1)} %get-tuple-element.74), channel_id=1, source_target_pairs={{0,2},{1,3},{2,0},{3,1},{4,6},{5,7},{6,4},{7,5},{8,10},{9,11},{10,... | collective-permute-start | bytes 196616 | tf_op jit(solution)/shard_map/ppermute | solution.py:20
  144.3 3.7 %collective-permute-start.14 = (bf16[32,1024]{1,0:T(8,128)(2,1)S(1)}, bf16[32,1024]{1,0:T(8,128)(2,1)S(1)}, u32[]{:S(2)}, u32[]{:S(2)}) collective-permute-start(bf16[32,1024]{1,0:T(8,128)(2,1)S(1)} %get-tuple-element.75), channel_id=1, source_target_pairs={{0,3},{1,0},{2,1},{3,2},{4,7},{5,4},{6,5},{7,6},{8,11},{9,8},{10,9... | collective-permute-start | bytes 196616 | tf_op jit(solution)/shard_map/ppermute | solution.py:20
  145.3 4.3 %collective-permute-start.13 = (bf16[32,1024]{1,0:T(8,128)(2,1)S(1)}, bf16[32,1024]{1,0:T(8,128)(2,1)S(1)}, u32[]{:S(2)}, u32[]{:S(2)}) collective-permute-start(bf16[32,1024]{1,0:T(8,128)(2,1)S(1)} %get-tuple-element.73), channel_id=1, source_target_pairs={{0,1},{1,2},{2,3},{3,0},{4,5},{5,6},{6,7},{7,4},{8,9},{9,10},{10,1... | collective-permute-start | bytes 196616 | tf_op jit(solution)/shard_map/ppermute | solution.py:20
  150.8 6.0 %copy-start.30 = (s32[1,1024]{1,0:T(1,128)S(1)}, s32[1,1024]{1,0:T(1,128)}, u32[]{:S(2)}) copy-start(s32[1,1024]{1,0:T(1,128)} %copy-done.29) | copy-start | bytes 12292
  150.8 6.0 %copy-start.10 = (f32[768,384]{1,0:T(8,128)S(1)}, f32[768,384]{1,0:T(8,128)}, u32[]{:S(2)}) copy-start(f32[768,384]{1,0:T(8,128)} %copy-done.9) | copy-start | bytes 3538948
  150.8 6.0 %copy-start.12 = (f32[768,384]{1,0:T(8,128)S(1)}, f32[768,384]{1,0:T(8,128)}, u32[]{:S(2)}) copy-start(f32[768,384]{1,0:T(8,128)} %copy-done.11) | copy-start | bytes 3538948
  154.1 9.5 %collective-permute-start.16 = (bf16[256,1024]{1,0:T(8,128)(2,1)}, bf16[256,1024]{1,0:T(8,128)(2,1)S(1)}, u32[]{:S(2)}, u32[]{:S(2)}) collective-permute-start(bf16[256,1024]{1,0:T(8,128)(2,1)} %get-tuple-element.53), channel_id=1, source_target_pairs={{0,1},{1,2},{2,3},{3,0},{4,5},{5,6},{6,7},{7,4},{8,9},{9,10},{10,1... | collective-permute-start | bytes 1572872 | tf_op jit(solution)/shard_map/ppermute | solution.py:20
  154.1 9.5 %collective-permute-start.17 = (bf16[256,1024]{1,0:T(8,128)(2,1)}, bf16[256,1024]{1,0:T(8,128)(2,1)}, u32[]{:S(2)}, u32[]{:S(2)}) collective-permute-start(bf16[256,1024]{1,0:T(8,128)(2,1)} %get-tuple-element.54), channel_id=1, source_target_pairs={{0,3},{1,0},{2,1},{3,2},{4,7},{5,4},{6,5},{7,6},{8,11},{9,8},{10,9... | collective-permute-start | bytes 1572872 | tf_op jit(solution)/shard_map/ppermute | solution.py:20
  168.2 29.8 %collective-permute-start.18 = (bf16[2,256,1024]{2,1,0:T(8,128)(2,1)}, bf16[2,256,1024]{2,1,0:T(8,128)(2,1)S(1)}, u32[]{:S(2)}, u32[]{:S(2)}) collective-permute-start(bf16[2,256,1024]{2,1,0:T(8,128)(2,1)} %get-tuple-element.55), channel_id=1, source_target_pairs={{0,1},{1,2},{2,3},{3,0},{4,5},{5,6},{6,7},{7,4},{8,9},{9,10},{10,1... | collective-permute-start | bytes 3145736 | tf_op jit(solution)/shard_map/ppermute | solution.py:20
  168.2 29.8 %collective-permute-start.19 = (bf16[2,256,1024]{2,1,0:T(8,128)(2,1)}, bf16[2,256,1024]{2,1,0:T(8,128)(2,1)S(1)}, u32[]{:S(2)}, u32[]{:S(2)}) collective-permute-start(bf16[2,256,1024]{2,1,0:T(8,128)(2,1)} %get-tuple-element.56), channel_id=1, source_target_pairs={{0,3},{1,0},{2,1},{3,2},{4,7},{5,4},{6,5},{7,6},{8,11},{9,8},{10,9... | collective-permute-start | bytes 3145736 | tf_op jit(solution)/shard_map/ppermute | solution.py:20
  174.0 24.0 %collective-permute-start.20 = (bf16[256,1024]{1,0:T(8,128)(2,1)}, bf16[256,1024]{1,0:T(8,128)(2,1)S(1)}, u32[]{:S(2)}, u32[]{:S(2)}) collective-permute-start(bf16[256,1024]{1,0:T(8,128)(2,1)} %get-tuple-element.57), channel_id=1, source_target_pairs={{0,1},{1,2},{2,3},{3,0},{4,5},{5,6},{6,7},{7,4},{8,9},{9,10},{10,1... | collective-permute-start | bytes 1572872 | tf_op jit(solution)/shard_map/ppermute | solution.py:20
  174.0 24.0 %collective-permute-start.21 = (bf16[256,1024]{1,0:T(8,128)(2,1)}, bf16[256,1024]{1,0:T(8,128)(2,1)S(1)}, u32[]{:S(2)}, u32[]{:S(2)}) collective-permute-start(bf16[256,1024]{1,0:T(8,128)(2,1)} %get-tuple-element.58), channel_id=1, source_target_pairs={{0,3},{1,0},{2,1},{3,2},{4,7},{5,4},{6,5},{7,6},{8,11},{9,8},{10,9... | collective-permute-start | bytes 1572872 | tf_op jit(solution)/shard_map/ppermute | solution.py:20
  198.0 1.6 copy-start.20
  203.0 52.2 %all-to-all-start.2 = ((bf16[64,8,1024]{2,1,0:T(8,128)(2,1)}), bf16[64,8,1024]{2,1,0:T(8,128)(2,1)S(1)}, u32[]{:S(2)}, u32[]{:S(2)}) async-start(bf16[64,8,1024]{2,1,0:T(8,128)(2,1)} %bitcast.70), calls=%async_computation.2 | async-start | bytes 2097152 | tf_op jit(solution)/shard_map/all_to_all | solution.py:33
  223.9 25.8 %collective-permute-start.22 = (bf16[2,256,1024]{2,1,0:T(8,128)(2,1)}, bf16[2,256,1024]{2,1,0:T(8,128)(2,1)S(1)}, u32[]{:S(2)}, u32[]{:S(2)}) collective-permute-start(bf16[2,256,1024]{2,1,0:T(8,128)(2,1)} %get-tuple-element.59), channel_id=1, source_target_pairs={{0,1},{1,2},{2,3},{3,0},{4,5},{5,6},{6,7},{7,4},{8,9},{9,10},{10,1... | collective-permute-start | bytes 3145736 | tf_op jit(solution)/shard_map/ppermute | solution.py:20
  223.9 25.8 %collective-permute-start.23 = (bf16[2,256,1024]{2,1,0:T(8,128)(2,1)}, bf16[2,256,1024]{2,1,0:T(8,128)(2,1)S(1)}, u32[]{:S(2)}, u32[]{:S(2)}) collective-permute-start(bf16[2,256,1024]{2,1,0:T(8,128)(2,1)} %get-tuple-element.60), channel_id=1, source_target_pairs={{0,3},{1,0},{2,1},{3,2},{4,7},{5,4},{6,5},{7,6},{8,11},{9,8},{10,9... | collective-permute-start | bytes 3145736 | tf_op jit(solution)/shard_map/ppermute | solution.py:20
  255.1 11.2 %copy-start.31 = (f32[16,8]{0,1:T(8,128)S(1)}, f32[16,8]{0,1:T(8,128)}, u32[]{:S(2)}) copy-start(f32[16,8]{0,1:T(8,128)} %param.12) | copy-start | bytes 1540
  255.1 12.7 %copy-start.33 = (s32[64]{0:T(128)S(1)}, s32[64]{0:T(128)}, u32[]{:S(2)}) copy-start(s32[64]{0:T(128)} %copy-done.32) | copy-start | bytes 772
  255.1 12.9 %copy-start.24 = (s32[64,32]{1,0:T(8,128)S(1)}, s32[64,32]{1,0:T(8,128)}, u32[]{:S(2)}) copy-start(s32[64,32]{1,0:T(8,128)} %copy-done.23) | copy-start | bytes 24580
  255.1 12.9 %copy-start.28 = (s32[512]{0:T(512)S(1)}, s32[512]{0:T(512)}, u32[]{:S(2)}) copy-start(s32[512]{0:T(512)} %copy-done.27) | copy-start | bytes 6148
  255.2 40.8 %all-to-all-start.3 = ((bf16[64,8,1024]{2,1,0:T(8,128)(2,1)}), bf16[64,8,1024]{2,1,0:T(8,128)(2,1)S(1)}, u32[]{:S(2)}, u32[]{:S(2)}) async-start(bf16[64,8,1024]{2,1,0:T(8,128)(2,1)} %bitcast.71), calls=%async_computation.3 | async-start | bytes 2097152 | tf_op jit(solution)/shard_map/all_to_all | solution.py:33
  266.4 1.3 collective-permute-start.1
  296.7 2.0 collective-permute-start.24
  (17 other events, 15.5 us)
